TPU v7x, 512 devices: a whole 4x8x8 slice. The times are simulated.
512 devices in a mesh: grp: 8 (over z), seq: 64 (over y, x, core).
Axes of the slice: x: 4, y: 8, z: 8, core: 2. Of those that a mesh axis runs over, the one named last changes fastest.
Arguments:
- rows: bfloat16 [8, 4096, 3, 4096], P('grp', 'seq'), may hold values from -6 to 6
- lengths: int32 [8], P('grp'), may hold values from 512 to 4096, as said below
- short_weight: float32 [3, 3, 4096], replicated, may hold values from -3 to 3
- long_filter: float32 [4096, 4096], P('seq', 'grp')
- filter_bias: float32 [4096], P('seq'), may hold values from -4 to 4
Outputs:
- mixed: bfloat16 [8, 4096, 4096], P('grp', 'seq')
Inputs may be any that keep to these rules, and one draw needn't show every extreme that they name: `lengths`: in every draw some sequence has length 4096.
All inputs are finite; a program needn't handle non-finite values.
Results may differ from a plain program's by a relative error of at most 0.0057.
Values may be sent and summed in bfloat16 or wider, within the bound.
No kernel may reach another device: no remote copies, remote signals or barrier semaphores. Data moves between devices by JAX's collectives and lax.ppermute only.
A program may use at most 64 MiB of HBM per device.

v0:
```python
import math

import jax
import jax.numpy as jnp
import numpy as np
from jax import lax
from jax.experimental import pallas as pl
from jax.experimental.pallas import tpu as pltpu
from jax.sharding import PartitionSpec as P

BF16 = jnp.bfloat16
F32 = jnp.float32
VMEM_BYTES = 48 * 1024 * 1024


def split_hi_lo(table):
    high = table.astype(jnp.bfloat16)
    low = (table - high.astype(np.float64)).astype(jnp.bfloat16)
    return np.concatenate([high, low], axis=1)


def transform_tables(na, nb):
    n = na * nb
    a = np.arange(na)
    b = np.arange(nb)
    k1 = np.arange(na)
    angle = 2.0 * math.pi * np.outer(k1 + 0.25, a) / na
    first = np.concatenate([np.cos(angle), -np.sin(angle)], axis=0)
    order = np.concatenate([k1[0::2], k1[1::2]])
    back = 2.0 * math.pi * np.outer(a, order + 0.25) / na
    first_back = np.concatenate([np.cos(back), -np.sin(back)], axis=1)
    inner = 2.0 * math.pi * np.outer(b, b) / nb
    cos, sin = np.cos(inner), np.sin(inner)
    second = np.block([[cos, sin], [-sin, cos]])
    second_back = np.block([[cos, -sin], [sin, cos]])
    turn = 2.0 * math.pi * (k1[:, None] + 0.25) * b[None, :] / n
    turn = turn.reshape(na // 2, 2, nb).transpose(0, 2, 1)
    turn = np.repeat(turn, 64, axis=2)
    return (
        split_hi_lo(first),
        split_hi_lo(second),
        split_hi_lo(second_back),
        split_hi_lo(first_back),
        np.cos(turn).astype(np.float32),
        (-np.sin(turn)).astype(np.float32),
    )


def swap_halves(x):
    return pltpu.roll(x, 64, axis=1)


def lane_mix(one, two):
    low = lax.broadcasted_iota(jnp.int32, one.shape, 1) < 64
    return (
        jnp.where(low, one, swap_halves(two)),
        jnp.where(low, swap_halves(one), two),
    )


def twice(x):
    return jnp.concatenate([x, x], axis=0)


def dot(table, x):
    return jnp.dot(table, x, preferred_element_type=F32)


def block_stage(data32, mid, first, na, nr):
    for r in range(0, nr, 2):
        one = data32[pl.ds(r, na, stride=nr), :]
        two = data32[pl.ds(r + 1, na, stride=nr), :]
        both = jnp.concatenate([one, two], axis=1).astype(BF16)
        got = dot(first, twice(both))
        mid[pl.ds(r * 2 * na, 2 * na), :] = got[:, :128]
        mid[pl.ds((r + 1) * 2 * na, 2 * na), :] = got[:, 128:]


def turned(mid, turn_re, turn_im, p, na, nr):
    parts = []
    for ri in range(2):
        one = mid[pl.ds(ri * na + 2 * p, nr, stride=2 * na), :]
        two = mid[pl.ds(ri * na + 2 * p + 1, nr, stride=2 * na), :]
        top, bottom = lane_mix(one, two)
        parts.append(jnp.concatenate([top, bottom], axis=0))
    re, im = parts
    tre, tim = turn_re[p], turn_im[p]
    return re * tre - im * tim, re * tim + im * tre


def filter_kernel(filt, first, second, turn_re, turn_im, spec, data32, mid):
    na, nr, _ = filt.shape
    nb = 2 * nr
    data32[...] = filt[...].astype(F32).reshape(na * nr, 128)
    first, second = first[...], second[...]
    block_stage(data32, mid, first, na, nr)
    for p in range(0, na // 2, 2):
        cols = []
        for q in (p, p + 1):
            re, im = turned(mid, turn_re, turn_im, q, na, nr)
            cols.append(jnp.concatenate([re, im], axis=0))
        both = jnp.concatenate(cols, axis=1)
        high = both.astype(BF16)
        low = (both - high.astype(F32)).astype(BF16)
        got = dot(second, twice(high)) + dot(second[:, : 2 * nb], low)
        got = got * (1.0 / (na * nb))
        spec[p] = got[:, :128]
        spec[p + 1] = got[:, 128:]


def conv_kernel(z, spec, bias, first, second, second_back, first_back, turn_re, turn_im, out, data32, mid, mid_back):
    na, nr, _ = z.shape
    nb = 2 * nr
    data32[...] = z[...].astype(F32).reshape(na * nr, 128)
    first, second, second_back, first_back = first[...], second[...], second_back[...], first_back[...]
    block_stage(data32, mid, first, na, nr)
    for p in range(0, na // 2, 2):
        cols = []
        for q in (p, p + 1):
            re, im = turned(mid, turn_re, turn_im, q, na, nr)
            cols.append(jnp.concatenate([re, im], axis=0))
        got = dot(second, twice(jnp.concatenate(cols, axis=1).astype(BF16)))
        cols = []
        for j, q in enumerate((p, p + 1)):
            re, im = got[:nb, j * 128 : (j + 1) * 128], got[nb:, j * 128 : (j + 1) * 128]
            sre, sim = spec[q, pl.ds(0, nb), :], spec[q, pl.ds(nb, nb), :]
            cols.append(jnp.concatenate([re * sre - im * sim, re * sim + im * sre], axis=0))
        got = dot(second_back, twice(jnp.concatenate(cols, axis=1).astype(BF16)))
        for j, q in enumerate((p, p + 1)):
            re, im = got[:nb, j * 128 : (j + 1) * 128], got[nb:, j * 128 : (j + 1) * 128]
            tre, tim = turn_re[q], turn_im[q]
            mid_back[pl.ds(q * 2 * nb, nb), :] = re * tre + im * tim
            mid_back[pl.ds(q * 2 * nb + nb, nb), :] = im * tre - re * tim
    gain = bias[...]
    for r in range(0, nr, 2):
        cols = []
        for s in (r, r + 1):
            parts = []
            for ri in range(2):
                one = mid_back[pl.ds(ri * nb + s, na // 2, stride=2 * nb), :]
                two = mid_back[pl.ds(ri * nb + s + nr, na // 2, stride=2 * nb), :]
                parts.extend(lane_mix(one, two))
            cols.append(jnp.concatenate(parts, axis=0))
        got = dot(first_back, twice(jnp.concatenate(cols, axis=1).astype(BF16)))
        for j, s in enumerate((r, r + 1)):
            at = pl.ds(s, na, stride=nr)
            data32[at, :] = got[:, j * 128 : (j + 1) * 128] + gain * data32[at, :]
    out[...] = data32[...].reshape(na, nr, 128).astype(BF16)


def turn_filter_kernel(filt, out):
    for i in range(out.shape[0] // 2):
        block = filt[:, i * 128 : (i + 1) * 128].T
        for j in range(2):
            part = block[j * 64 : (j + 1) * 64]
            out[2 * i + j] = jnp.concatenate([part[:32], part[32:]], axis=1).astype(BF16)


def short_sum(x, halo, weights, alive):
    tok, width = x.shape
    row = lax.broadcasted_iota(jnp.int32, (tok, width), 0)
    x = jnp.where(row < alive, x.astype(F32), 0.0)
    halo = halo.astype(F32)
    before2 = jnp.where(alive > -2, halo[0:1], 0.0)
    before1 = jnp.where(alive > -1, halo[1:2], 0.0)
    back1 = jnp.where(row == 0, before1, pltpu.roll(x, 1, axis=0))
    back2 = jnp.where(row == 0, before2, jnp.where(row == 1, before1, pltpu.roll(x, 2, axis=0)))
    return weights[0:1] * x + weights[1:2] * back1 + weights[2:3] * back2


def gate_kernel(alive, rows, halo, weights, out):
    for i in range(rows.shape[2] // 128):
        at = pl.ds(i * 128, 128)
        key = short_sum(rows[0, :, at], halo[0, :, at], weights[0, :, at], alive[0])
        val = short_sum(rows[1, :, at], halo[1, :, at], weights[1, :, at], alive[0])
        z = key * val
        half = z.shape[0] // 2
        one, two = lane_mix(z[:half], z[half:])
        out[2 * i] = one.astype(BF16)
        out[2 * i + 1] = two.astype(BF16)


def query_kernel(alive, rows, halo, weights, out):
    for i in range(rows.shape[2] // 128):
        at = pl.ds(i * 128, 128)
        query = short_sum(rows[0, :, at], halo[0, :, at], weights[0, :, at], alive[0])
        row = lax.broadcasted_iota(jnp.int32, query.shape, 0)
        out[:, at] = jnp.where(row < alive[0], query, 0.0)


def mix_kernel(y, query, out):
    for i in range(out.shape[1] // 128):
        at = pl.ds(i * 128, 128)
        top, bottom = lane_mix(y[2 * i].astype(F32), y[2 * i + 1].astype(F32))
        out[:, at] = (query[:, at] * jnp.concatenate([top, bottom], axis=0)).astype(BF16)


def vmem(count):
    return [pl.BlockSpec(memory_space=pltpu.VMEM)] * count


def params():
    return pltpu.CompilerParams(vmem_limit_bytes=VMEM_BYTES)


def per_device(rows, lengths, short_weight, long_filter, filter_bias):
    tok, width = rows.shape[1], rows.shape[3]
    nseq = lax.axis_size("seq")
    ngrp = lax.axis_size("grp")
    me = lax.axis_index("seq")
    chans = width // nseq
    half = tok // 2
    span = long_filter.shape[1]
    parts = jnp.transpose(rows[0], (1, 0, 2))
    alive = lengths - me * tok
    halo = lax.ppermute(parts[:, tok - 2 :, :], "seq", [(i, i + 1) for i in range(nseq - 1)])
    tables = [jnp.asarray(t) for t in transform_tables(nseq, tok)]
    first, second, second_back, first_back, turn_re, turn_im = tables

    own = pl.pallas_call(
        turn_filter_kernel,
        out_shape=jax.ShapeDtypeStruct((span // tok, half, 2 * chans), BF16),
        in_specs=vmem(1),
        out_specs=pl.BlockSpec(memory_space=pltpu.VMEM),
        compiler_params=params(),
        name="turn_filter",
    )(long_filter)
    whole = lax.all_gather(own, "grp", axis=0, tiled=True)

    block = 1024
    z = pl.pallas_call(
        gate_kernel,
        grid=(width // block,),
        out_shape=jax.ShapeDtypeStruct((nseq, half, 2 * chans), BF16),
        in_specs=[
            pl.BlockSpec(memory_space=pltpu.SMEM),
            pl.BlockSpec((2, tok, block), lambda i: (0, 0, i)),
            pl.BlockSpec((2, 2, block), lambda i: (0, 0, i)),
            pl.BlockSpec((2, 3, block), lambda i: (0, 0, i)),
        ],
        out_specs=pl.BlockSpec((block // chans, half, 2 * chans), lambda i: (i, 0, 0)),
        compiler_params=params(),
        name="gate",
    )(alive, parts[1:], halo[1:], short_weight[1:])
    z = lax.all_to_all(z, "seq", split_axis=0, concat_axis=0, tiled=True)

    query = pl.pallas_call(
        query_kernel,
        grid=(width // block,),
        out_shape=jax.ShapeDtypeStruct((tok, width), F32),
        in_specs=[
            pl.BlockSpec(memory_space=pltpu.SMEM),
            pl.BlockSpec((1, tok, block), lambda i: (0, 0, i)),
            pl.BlockSpec((1, 2, block), lambda i: (0, 0, i)),
            pl.BlockSpec((1, 3, block), lambda i: (0, 0, i)),
        ],
        out_specs=pl.BlockSpec((tok, block), lambda i: (0, i)),
        compiler_params=params(),
        cost_estimate=pl.CostEstimate(flops=2000000, bytes_accessed=2000000, transcendentals=0),
        name="query",
    )(alive, parts, halo, short_weight)

    spec = pl.pallas_call(
        filter_kernel,
        out_shape=jax.ShapeDtypeStruct((nseq // 2, 2 * tok, 2 * chans), F32),
        in_specs=vmem(5),
        out_specs=pl.BlockSpec(memory_space=pltpu.VMEM),
        scratch_shapes=[
            pltpu.VMEM((nseq * half, 128), F32),
            pltpu.VMEM((half * 2 * nseq, 128), F32),
        ],
        compiler_params=params(),
        cost_estimate=pl.CostEstimate(flops=2000000000, bytes_accessed=6000000, transcendentals=0),
        name="filter_spectrum",
    )(whole, first, second, turn_re, turn_im)

    bias = jnp.tile(filter_bias, 2)[None]
    y = pl.pallas_call(
        conv_kernel,
        out_shape=jax.ShapeDtypeStruct((nseq, half, 2 * chans), BF16),
        in_specs=vmem(9),
        out_specs=pl.BlockSpec(memory_space=pltpu.VMEM),
        scratch_shapes=[
            pltpu.VMEM((nseq * half, 128), F32),
            pltpu.VMEM((half * 2 * nseq, 128), F32),
            pltpu.VMEM((nseq * tok, 128), F32),
        ],
        compiler_params=params(),
        name="convolve",
    )(z, spec, bias, first, second, second_back, first_back, turn_re, turn_im)
    y = lax.all_to_all(y, "seq", split_axis=0, concat_axis=0, tiled=True)

    block = 1024
    out = pl.pallas_call(
        mix_kernel,
        grid=(width // block,),
        out_shape=jax.ShapeDtypeStruct((tok, width), BF16),
        in_specs=[
            pl.BlockSpec((block // chans, half, 2 * chans), lambda i: (i, 0, 0)),
            pl.BlockSpec((tok, block), lambda i: (0, i)),
        ],
        out_specs=pl.BlockSpec((tok, block), lambda i: (0, i)),
        compiler_params=params(),
        name="mix",
    )(y, query)
    return out[None]


def solution(mesh):
    in_specs = (P("grp", "seq", None, None), P("grp"), P(), P("seq", "grp"), P("seq"))
    out_specs = P("grp", "seq", None)
    return jax.shard_map(
        per_device, mesh=mesh, in_specs=in_specs, out_specs=out_specs, check_vma=False
    )
```

profile of v0, /device:TPU:1, one launch (start us, length us, event | category | flops | bytes accessed | tf_op | source)
XLA Modules:
  0.0 99.9 jit_solution(6516995633011253327)
XLA Ops:
  0.0 0.0 copy-start.6
  0.0 1.0 %slice.17 = bf16[3,2,4096]{2,1,0:T(2,128)(2,1)S(1)} slice(bf16[3,64,4096]{2,1,0:T(8,128)(2,1)} %bitcast.5), slice={[0:3], [62:64], [0:4096]} | slice | bytes 98304 | tf_op jit(solution)/shard_map/slice | solution.py:216
  1.0 0.0 copy-start.7
  1.0 4.6 %collective-permute-start = (bf16[3,2,4096]{2,1,0:T(2,128)(2,1)S(1)}, bf16[3,2,4096]{2,1,0:T(2,128)(2,1)S(1)}, u32[]{:S(2)}, u32[]{:S(2)}) collective-permute-start(bf16[3,2,4096]{2,1,0:T(2,128)(2,1)S(1)} %slice.17), channel_id=1, source_target_pairs={{0,1},{1,2},{2,3},{3,4},{4,5},{5,6},{6,7},{7,8},{8,9},{9,10},{10,1... | collective-permute-start | bytes 147464 | tf_op jit(solution)/shard_map/ppermute | solution.py:216
  5.7 1.3 %slice.16.rows = bf16[2,64,4096]{2,1,0:T(8,128)(2,1)S(1)} slice(bf16[3,64,4096]{2,1,0:T(8,128)(2,1)} %bitcast.6), slice={[1:3], [0:64], [0:4096]} | slice | bytes 2097152 | tf_op jit(solution)/shard_map/slice | solution.py:244
  7.0 0.0 copy-start.13
  7.0 0.0 copy-start.3
  7.0 0.0 copy-start.8
  7.0 0.0 copy-start.10
  7.8 0.0 copy-done.6
  7.8 2.2 %collective-permute-done.halo = bf16[3,2,4096]{2,1,0:T(2,128)(2,1)S(1)} collective-permute-done((bf16[3,2,4096]{2,1,0:T(2,128)(2,1)S(1)}, bf16[3,2,4096]{2,1,0:T(2,128)(2,1)S(1)}, u32[]{:S(2)}, u32[]{:S(2)}) %collective-permute-start) | collective-permute-done | bytes 49184 | tf_op jit(solution)/shard_map/ppermute | solution.py:216
  10.1 2.4 %gate.1 = bf16[64,32,128]{2,1,0:T(8,128)(2,1)} custom-call(s32[1]{0:T(128)S(6)} %sub.7.alive, bf16[2,64,4096]{2,1,0:T(8,128)(2,1)S(1)} %slice.16.rows, bf16[2,2,4096]{2,1,0:T(2,128)(2,1)S(1)} %slice.18.halo, f32[2,3,4096]{2,1,0:T(4,128)S(1)} %slice.15.weights), custom_call_target="tpu_custom_call" | custom-call | tf_op jit(solution)/shard_map/gate/pallas_call | solution.py:231
  12.4 9.0 %all-to-all-start = ((bf16[64,32,128]{2,1,0:T(8,128)(2,1)}), bf16[64,32,128]{2,1,0:T(8,128)(2,1)S(1)}, u32[]{:S(2)}, u32[]{:S(2)}) async-start(bf16[64,32,128]{2,1,0:T(8,128)(2,1)} %gate.1), calls=%async_computation | async-start | bytes 1048576 | tf_op jit(solution)/shard_map/all_to_all | solution.py:245
  21.4 0.0 copy-done.7
  21.5 0.2 turn_filter.1
  21.7 0.0 copy-done.13
  21.7 0.6 broadcast_in_dim_tile.3.bias
  22.3 26.8 %all_gather.3.filt = bf16[64,32,128]{2,1,0:T(8,128)(2,1)S(1)} all-gather(bf16[8,32,128]{2,1,0:T(8,128)(2,1)S(1)} %turn_filter.1), channel_id=1, replica_groups=mesh['grp'=8,'seq'=64] {'grp'}, dimensions={0}, use_global_device_ids=true | all-gather | bytes 589824 | tf_op jit(solution)/shard_map/all_gather | solution.py:228
  49.1 0.0 copy-done.3
  49.1 0.0 copy-done.8
  49.1 0.0 copy-done.10
  49.1 0.0 copy-start.4
  49.2 1.2 %copy-done.4 = f32[32,64,128]{2,1,0:T(8,128)S(1)} copy-done((f32[32,64,128]{2,1,0:T(8,128)S(1)}, f32[32,64,128]{2,1,0:T(8,128)}, u32[]{:S(2)}) %copy-start.4) | copy-done | bytes 1048600
  50.4 0.0 copy-start.9
  50.4 2.8 %filter_spectrum.1.spec = f32[32,128,128]{2,1,0:T(8,128)S(1)} custom-call(bf16[64,32,128]{2,1,0:T(8,128)(2,1)S(1)} %all_gather.3.filt, bf16[128,128]{1,0:T(8,128)(2,1)S(1)} %copy-done.10, bf16[128,256]{1,0:T(8,128)(2,1)S(1)} %copy-done.8, f32[32,64,128]{2,1,0:T(8,128)S(1)} %copy-done.3, f32[32,64,128]{2,1,0:T(8,128)S(1)} %copy-done.4), custom_call_target="tpu_custom_call" | custom-call | flops 2000000000 | bytes 6000000 | tf_op jit(solution)/shard_map/filter_spectrum/pallas_call | solution.py:263
  53.1 0.0 copy-start.1
  53.2 1.3 %copy-done.1 = f32[32,128,128]{2,1,0:T(8,128)} copy-done((f32[32,128,128]{2,1,0:T(8,128)}, f32[32,128,128]{2,1,0:T(8,128)S(1)}, u32[]{:S(2)}) %copy-start.1) | copy-done | bytes 2097176
  54.5 0.0 copy-start
  54.5 0.0 all-to-all-done.z
  54.5 0.0 copy-done.9
  54.5 0.0 copy-start.2
  54.5 1.7 %copy-done.2 = f32[32,128,128]{2,1,0:T(8,128)S(1)} copy-done((f32[32,128,128]{2,1,0:T(8,128)S(1)}, f32[32,128,128]{2,1,0:T(8,128)}, u32[]{:S(2)}) %copy-start.2) | copy-done | bytes 2097176
  56.2 0.0 copy-start.5
  56.2 1.2 %copy-done.5 = f32[32,64,128]{2,1,0:T(8,128)S(1)} copy-done((f32[32,64,128]{2,1,0:T(8,128)S(1)}, f32[32,64,128]{2,1,0:T(8,128)}, u32[]{:S(2)}) %copy-start.5) | copy-done | bytes 1048600
  57.4 0.0 copy-start.11
  57.4 0.8 copy-done.11
  58.2 0.0 copy-start.12
  58.2 0.6 copy-done.12
  58.8 6.5 %convolve.1 = bf16[64,32,128]{2,1,0:T(8,128)(2,1)} custom-call(bf16[64,32,128]{2,1,0:T(8,128)(2,1)S(1)} %all-to-all-done.z, f32[32,128,128]{2,1,0:T(8,128)S(1)} %copy-done.2, f32[1,128]{1,0:T(1,128)S(1)} %copy-done.12, bf16[128,128]{1,0:T(8,128)(2,1)S(1)} %copy-done.10, bf16[128,256]{1,0:T(8,128)(2,1)S(1)} %copy-done.8, bf16[128,256]{1,0:T(8,128)(2,1)S(1)} %copy-done.9, ...), custom_call_target="tpu_custom_call" | custom-call | tf_op jit(solution)/shard_map/convolve/pallas_call | solution.py:278
  65.3 15.1 %all-to-all-start.1 = ((bf16[64,32,128]{2,1,0:T(8,128)(2,1)}), bf16[64,32,128]{2,1,0:T(8,128)(2,1)S(1)}, u32[]{:S(2)}, u32[]{:S(2)}) async-start(bf16[64,32,128]{2,1,0:T(8,128)(2,1)} %convolve.1), calls=%async_computation.1 | async-start | bytes 1048576 | tf_op jit(solution)/shard_map/all_to_all | solution.py:291
  80.4 0.0 copy-done
  80.4 0.6 query.1
  81.1 17.1 %all-to-all-done.1.y = bf16[64,32,128]{2,1,0:T(8,128)(2,1)S(1)} async-done(((bf16[64,32,128]{2,1,0:T(8,128)(2,1)}), bf16[64,32,128]{2,1,0:T(8,128)(2,1)S(1)}, u32[]{:S(2)}, u32[]{:S(2)}) %all-to-all-start.1) | async-done | bytes 524320 | tf_op jit(solution)/shard_map/all_to_all | solution.py:291
  98.1 1.8 %mix.1 = bf16[64,4096]{1,0:T(8,128)(2,1)} custom-call(bf16[64,32,128]{2,1,0:T(8,128)(2,1)S(1)} %all-to-all-done.1.y, f32[64,4096]{1,0:T(8,128)S(1)} %query.1), custom_call_target="tpu_custom_call" | custom-call | tf_op jit(solution)/shard_map/mix/pallas_call | solution.py:294
  (3 shorter events, 0.1 us)
Async XLA Ops:
  0.0 7.8 %copy-start.6 = (f32[3,3,4096]{2,1,0:T(4,128)S(1)}, f32[3,3,4096]{2,1,0:T(4,128)}, u32[]{:S(2)}) copy-start(f32[3,3,4096]{2,1,0:T(4,128)} %weights.1) | copy-start | bytes 442372
  1.0 20.4 %copy-start.7 = (f32[64,512]{1,0:T(8,128)S(1)}, f32[64,512]{1,0:T(8,128)}, u32[]{:S(2)}) copy-start(f32[64,512]{1,0:T(8,128)} %filt.1) | copy-start | bytes 393220
  1.0 9.0 %collective-permute-start = (bf16[3,2,4096]{2,1,0:T(2,128)(2,1)S(1)}, bf16[3,2,4096]{2,1,0:T(2,128)(2,1)S(1)}, u32[]{:S(2)}, u32[]{:S(2)}) collective-permute-start(bf16[3,2,4096]{2,1,0:T(2,128)(2,1)S(1)} %slice.17), channel_id=1, source_target_pairs={{0,1},{1,2},{2,3},{3,4},{4,5},{5,6},{6,7},{7,8},{8,9},{9,10},{10,1... | collective-permute-start | bytes 147464 | tf_op jit(solution)/shard_map/ppermute | solution.py:216
  7.0 14.7 %copy-start.13 = (f32[64]{0:T(128)S(1)}, f32[64]{0:T(128)}, u32[]{:S(2)}) copy-start(f32[64]{0:T(128)} %param.15) | copy-start | bytes 772
  7.0 42.1 %copy-start.3 = (f32[32,64,128]{2,1,0:T(8,128)S(1)}, f32[32,64,128]{2,1,0:T(8,128)}, u32[]{:S(2)}) copy-start(f32[32,64,128]{2,1,0:T(8,128)} %constant.22.clone.turn_re) | copy-start | bytes 3145732
  7.0 42.1 %copy-start.8 = (bf16[128,256]{1,0:T(8,128)(2,1)S(1)}, bf16[128,256]{1,0:T(8,128)(2,1)}, u32[]{:S(2)}) copy-start(bf16[128,256]{1,0:T(8,128)(2,1)} %constant.19.clone.second) | copy-start | bytes 196612
  7.0 42.1 %copy-start.10 = (bf16[128,128]{1,0:T(8,128)(2,1)S(1)}, bf16[128,128]{1,0:T(8,128)(2,1)}, u32[]{:S(2)}) copy-start(bf16[128,128]{1,0:T(8,128)(2,1)} %constant.18.clone.first) | copy-start | bytes 98308
  12.4 42.1 %all-to-all-start = ((bf16[64,32,128]{2,1,0:T(8,128)(2,1)}), bf16[64,32,128]{2,1,0:T(8,128)(2,1)S(1)}, u32[]{:S(2)}, u32[]{:S(2)}) async-start(bf16[64,32,128]{2,1,0:T(8,128)(2,1)} %gate.1), calls=%async_computation | async-start | bytes 1048576 | tf_op jit(solution)/shard_map/all_to_all | solution.py:245
  49.1 1.2 %copy-start.4 = (f32[32,64,128]{2,1,0:T(8,128)S(1)}, f32[32,64,128]{2,1,0:T(8,128)}, u32[]{:S(2)}) copy-start(f32[32,64,128]{2,1,0:T(8,128)} %constant.23.clone.turn_im) | copy-start | bytes 3145732
  50.4 4.1 %copy-start.9 = (bf16[128,256]{1,0:T(8,128)(2,1)S(1)}, bf16[128,256]{1,0:T(8,128)(2,1)}, u32[]{:S(2)}) copy-start(bf16[128,256]{1,0:T(8,128)(2,1)} %constant.20.clone.second_back) | copy-start | bytes 196612
  53.1 1.3 %copy-start.1 = (f32[32,128,128]{2,1,0:T(8,128)}, f32[32,128,128]{2,1,0:T(8,128)S(1)}, u32[]{:S(2)}) copy-start(f32[32,128,128]{2,1,0:T(8,128)S(1)} %filter_spectrum.1.spec) | copy-start | bytes 6291460
  54.5 25.9 %copy-start = (bf16[1,64,3,4096]{3,1,2,0:T(8,128)(2,1)S(1)}, bf16[1,64,3,4096]{3,1,2,0:T(8,128)(2,1)}, u32[]{:S(2)}) copy-start(bf16[1,64,3,4096]{3,1,2,0:T(8,128)(2,1)} %param.11) | copy-start | bytes 4718596
  54.5 1.7 %copy-start.2 = (f32[32,128,128]{2,1,0:T(8,128)S(1)}, f32[32,128,128]{2,1,0:T(8,128)}, u32[]{:S(2)}) copy-start(f32[32,128,128]{2,1,0:T(8,128)} %copy-done.1) | copy-start | bytes 6291460
  56.2 1.2 %copy-start.5 = (f32[32,64,128]{2,1,0:T(8,128)S(1)}, f32[32,64,128]{2,1,0:T(8,128)}, u32[]{:S(2)}) copy-start(f32[32,64,128]{2,1,0:T(8,128)} %constant.23.clone.turn_im) | copy-start | bytes 3145732
  57.4 0.8 copy-start.11
  58.2 0.6 copy-start.12
  65.3 32.8 %all-to-all-start.1 = ((bf16[64,32,128]{2,1,0:T(8,128)(2,1)}), bf16[64,32,128]{2,1,0:T(8,128)(2,1)S(1)}, u32[]{:S(2)}, u32[]{:S(2)}) async-start(bf16[64,32,128]{2,1,0:T(8,128)(2,1)} %convolve.1), calls=%async_computation.1 | async-start | bytes 1048576 | tf_op jit(solution)/shard_map/all_to_all | solution.py:291
where the time goes:
time: 100 us; the launch traced here: 99.9 us
  starting transfers between devices  28.8 us (29%)
  blocking collectives  26.8 us (27%)
  waiting for transfers between devices  19.3 us (19%)
  Pallas kernels  14.2 us (14%)
  local copies, waits for them, and re-layouts  9.84 us (10%)
    all_gather x1, blocking collectives, per_device(): whole = lax.all_gather(own, 'grp', axis=0, tiled=True)  26.8 us
    all_to_all x1, waiting for transfers between devices, per_device(): y = lax.all_to_all(y, 'seq', split_axis=0, concat_axis=0, tiled=True)  17.1 us
    all_to_all x1, starting transfers between devices, per_device(): y = lax.all_to_all(y, 'seq', split_axis=0, concat_axis=0, tiled=True)  15.1 us
    all_to_all x1, starting transfers between devices, per_device(): z = lax.all_to_all(z, 'seq', split_axis=0, concat_axis=0, tiled=True)  9.01 us
    unnamed x28, local copies, waits for them, and re-layouts  6.88 us
    pallas_call x1, Pallas kernels, per_device(): pl.pallas_call(conv_kernel, out_shape=jax.ShapeDtypeStruct((nseq, half, 2...  6.5 us
    ppermute x1, starting transfers between devices, per_device(): lax.ppermute(parts[:, tok - 2:, :], 'seq', [(i, i + 1) for i in range(nse...  4.64 us
    pallas_call x1, Pallas kernels, per_device(): pl.pallas_call(filter_kernel, out_shape=jax.ShapeDtypeStruct((nseq // 2,...  2.76 us
  transfers between devices with their start and end apart: 3, of which 2 were waited for; matrix products, arithmetic and copies ran while one was open for 2% of the time, Pallas kernels for 4%

commit v1 on v0

v1 whole, which is shorter than its diff:
```python
import math

import jax
import jax.numpy as jnp
import numpy as np
from jax import lax
from jax.experimental import pallas as pl
from jax.experimental.pallas import tpu as pltpu
from jax.sharding import PartitionSpec as P

BF16 = jnp.bfloat16
F32 = jnp.float32
FINE = 4
PAD = 4


def split_hi_lo(table):
    high = table.astype(jnp.bfloat16)
    low = (table - high.astype(np.float64)).astype(jnp.bfloat16)
    return np.concatenate([high, low], axis=1)


def transform_tables(na, nb):
    n = na * nb
    a = np.arange(na)
    b = np.arange(nb)
    k1 = np.arange(na)
    angle = 2.0 * math.pi * np.outer(k1 + 0.25, a) / na
    first = np.concatenate([np.cos(angle), -np.sin(angle)], axis=0)
    order = np.concatenate([k1[0::2], k1[1::2]])
    back = 2.0 * math.pi * np.outer(a, order + 0.25) / na
    first_back = np.concatenate([np.cos(back), -np.sin(back)], axis=1)
    inner = 2.0 * math.pi * np.outer(b, b) / nb
    cos, sin = np.cos(inner), np.sin(inner)
    second = np.block([[cos, sin], [-sin, cos]])
    second_back = np.block([[cos, -sin], [sin, cos]])
    turn = 2.0 * math.pi * (k1[:, None] + 0.25) * b[None, :] / n
    turn = turn.reshape(na // 2, 2, nb).transpose(0, 2, 1)
    turn = np.repeat(turn, 64, axis=2)
    mats = [first, second, second_back, first_back]
    mats = [split_hi_lo(m) for m in mats]
    mats = [np.pad(m, ((0, 0), (0, 4 * nb - m.shape[1]))) for m in mats]
    factors = np.concatenate([turn[::FINE], turn[:FINE] - turn[:1]], axis=0)
    turns = np.stack([np.cos(factors), -np.sin(factors)]).astype(np.float32)
    return np.concatenate(mats, axis=0), turns


def swap_halves(x):
    return pltpu.roll(x, 64, axis=1)


def lane_mix(one, two):
    low = lax.broadcasted_iota(jnp.int32, one.shape, 1) < 64
    return (
        jnp.where(low, one, swap_halves(two)),
        jnp.where(low, swap_halves(one), two),
    )


def twice(x):
    return jnp.concatenate([x, x], axis=0)


def dot(table, x):
    return jnp.dot(table, x, preferred_element_type=F32)


def spread(data, data32):
    na, nr, _ = data.shape
    for a in range(na):
        data32[pl.ds(a * (nr + PAD), nr), :] = data[a].astype(F32)


def block_stage(data32, mid, first, na, nr):
    for r in range(0, nr, 2):
        one = data32[pl.ds(r, na, stride=nr + PAD), :]
        two = data32[pl.ds(r + 1, na, stride=nr + PAD), :]
        both = jnp.concatenate([one, two], axis=1).astype(BF16)
        got = dot(first, twice(both))
        mid[pl.ds(r * (2 * na + PAD), 2 * na), :] = got[:, :128]
        mid[pl.ds((r + 1) * (2 * na + PAD), 2 * na), :] = got[:, 128:]


def turn_of(turns, p):
    coarse = turns.shape[1] - FINE
    are, aim = turns[0, p // FINE], turns[1, p // FINE]
    if p % FINE == 0:
        return are, aim
    bre, bim = turns[0, coarse + p % FINE], turns[1, coarse + p % FINE]
    return are * bre - aim * bim, are * bim + aim * bre


def turned(mid, turn, p, na, nr):
    parts = []
    for ri in range(2):
        one = mid[pl.ds(ri * na + 2 * p, nr, stride=2 * na + PAD), :]
        two = mid[pl.ds(ri * na + 2 * p + 1, nr, stride=2 * na + PAD), :]
        top, bottom = lane_mix(one, two)
        parts.append(jnp.concatenate([top, bottom], axis=0))
    re, im = parts
    tre, tim = turn
    return re * tre - im * tim, re * tim + im * tre


def copies(pairs, sems):
    made = [pltpu.make_async_copy(src, dst, sems.at[i]) for i, (src, dst) in enumerate(pairs)]
    for copy in made:
        copy.start()
    return made


def spec_parts(spec_in, spec, step):
    parts = [pl.ds(i, step) for i in range(0, spec.shape[0], step)]
    return [(spec_in.at[part], spec.at[part]) for part in parts]


def filter_kernel(place, own, across, one_on, one_back, bias, mats_in, turns_in, spec_out, data32, mid, spec, mats, turns, sems):
    na, nr = 4 * own.shape[0], own.shape[1]
    nb = 2 * nr
    step = na // 8
    made = copies([(mats_in, mats), (turns_in, turns)], sems)
    shards = 8
    rows = na // shards
    turned_round = 2 + 4 * lax.rem(place[0], 2)
    for source, start in ((own, 0), (across, turned_round), (one_on, 1), (one_back, 7)):
        for j in range(2):
            shard = lax.rem(place[0] + start + 4 * j, shards)
            base = pl.multiple_of(shard * (rows * (nr + PAD)), 8)
            for i in range(rows):
                data32[pl.ds(base + i * (nr + PAD), nr), :] = source[j * rows + i].astype(F32)
    made[0].wait()
    first = mats[0 : 2 * na, 0 : 2 * na]
    second = mats[2 * na : 2 * na + 2 * nb, :]
    block_stage(data32, mid, first, na, nr)
    made[1].wait()
    leaving = []
    delta = bias[...]
    delta = jnp.concatenate([delta, delta], axis=1)
    for p in range(0, na // 2, 2):
        cols, turn = [], []
        for q in (p, p + 1):
            turn.append(turn_of(turns, q))
            re, im = turned(mid, turn[-1], q, na, nr)
            cols.append(jnp.concatenate([re, im], axis=0))
        both = jnp.concatenate(cols, axis=1)
        high = both.astype(BF16)
        low = (both - high.astype(F32)).astype(BF16)
        got = dot(second, twice(high)) + dot(second[:, : 2 * nb], low)
        scale = 1.0 / (na * nb)
        for j, q in enumerate((p, p + 1)):
            spec[q, pl.ds(0, nb), :] = ((got[:nb, j * 128 : (j + 1) * 128] + delta) * scale).astype(BF16)
            spec[q, pl.ds(nb, nb), :] = (got[nb:, j * 128 : (j + 1) * 128] * scale).astype(BF16)
        if (p + 2) % step == 0:
            part = pl.ds(p + 2 - step, step)
            leave = pltpu.make_async_copy(spec.at[part], spec_out.at[part], sems.at[2 + p // step])
            leave.start()
            leaving.append(leave)
    for leave in leaving:
        leave.wait()


def conv_kernel(z, spec_in, mats_in, turns_in, out, data32, mid, mid_back, spec, mats, turns, sems):
    na, nr, _ = z.shape
    nb = 2 * nr
    step = na // 8
    made = copies([(mats_in, mats), (turns_in, turns)] + spec_parts(spec_in, spec, step), sems)
    spread(z, data32)
    made[0].wait()
    at = 2 * na
    first = mats[0:at, 0 : 2 * na]
    second = mats[at : at + 2 * nb, :]
    second_back = mats[at + 2 * nb : at + 4 * nb, :]
    first_back = mats[at + 4 * nb :, :]
    block_stage(data32, mid, first, na, nr)
    for p in range(0, na // 2, 2):
        if p == 0:
            made[1].wait()
        if p % step == 0:
            made[2 + p // step].wait()
        cols, turn = [], []
        for q in (p, p + 1):
            turn.append(turn_of(turns, q))
            re, im = turned(mid, turn[-1], q, na, nr)
            cols.append(jnp.concatenate([re, im], axis=0))
        got = dot(second, twice(jnp.concatenate(cols, axis=1).astype(BF16)))
        cols = []
        for j, q in enumerate((p, p + 1)):
            re, im = got[:nb, j * 128 : (j + 1) * 128], got[nb:, j * 128 : (j + 1) * 128]
            sre, sim = spec[q, pl.ds(0, nb), :].astype(F32), spec[q, pl.ds(nb, nb), :].astype(F32)
            cols.append(jnp.concatenate([re * sre - im * sim, re * sim + im * sre], axis=0))
        got = dot(second_back, twice(jnp.concatenate(cols, axis=1).astype(BF16)))
        for j, q in enumerate((p, p + 1)):
            re, im = got[:nb, j * 128 : (j + 1) * 128], got[nb:, j * 128 : (j + 1) * 128]
            tre, tim = turn[j]
            mid_back[pl.ds(q * (2 * nb + PAD), nb), :] = re * tre + im * tim
            mid_back[pl.ds(q * (2 * nb + PAD) + nb, nb), :] = im * tre - re * tim
    for r in range(0, nr, 2):
        cols = []
        for s in (r, r + 1):
            parts = []
            for ri in range(2):
                one = mid_back[pl.ds(ri * nb + s, na // 2, stride=2 * nb + PAD), :]
                two = mid_back[pl.ds(ri * nb + s + nr, na // 2, stride=2 * nb + PAD), :]
                parts.extend(lane_mix(one.astype(BF16), two.astype(BF16)))
            cols.append(jnp.concatenate(parts, axis=0))
        got = dot(first_back, twice(jnp.concatenate(cols, axis=1)))
        for j, s in enumerate((r, r + 1)):
            data32[pl.ds(s, na, stride=nr + PAD), :] = got[:, j * 128 : (j + 1) * 128]
    for a in range(na):
        out[a] = data32[pl.ds(a * (nr + PAD), nr), :].astype(BF16)


def turn_filter_kernel(filt, out):
    for i in range(out.shape[0] // 2):
        block = filt[:, i * 128 : (i + 1) * 128].T
        for j in range(2):
            part = block[j * 64 : (j + 1) * 64]
            out[2 * i + j] = jnp.concatenate([part[:32], part[32:]], axis=1).astype(BF16)


def short_sum(x, halo, weights, alive):
    tok, width = x.shape
    row = lax.broadcasted_iota(jnp.int32, (tok, width), 0)
    x = jnp.where(row < alive, x.astype(F32), 0.0)
    halo = halo.astype(F32)
    before2 = jnp.where(alive > -2, halo[0:1], 0.0)
    before1 = jnp.where(alive > -1, halo[1:2], 0.0)
    back1 = jnp.where(row == 0, before1, pltpu.roll(x, 1, axis=0))
    back2 = jnp.where(row == 0, before2, jnp.where(row == 1, before1, pltpu.roll(x, 2, axis=0)))
    return weights[0:1] * x + weights[1:2] * back1 + weights[2:3] * back2


def gate_kernel(alive, rows, halo, weights, out):
    for i in range(rows.shape[2] // 128):
        at = pl.ds(i * 128, 128)
        key = short_sum(rows[0, :, at], halo[1, :, at], weights[0, :, at], alive[0])
        val = short_sum(rows[1, :, at], halo[2, :, at], weights[1, :, at], alive[0])
        z = key * val
        half = z.shape[0] // 2
        one, two = lane_mix(z[:half], z[half:])
        out[2 * i] = one.astype(BF16)
        out[2 * i + 1] = two.astype(BF16)


def query_kernel(alive, rows, halo, weights, out):
    for i in range(rows.shape[2] // 128):
        at = pl.ds(i * 128, 128)
        query = short_sum(rows[0, :, at], halo[0, :, at], weights[0, :, at], alive[0])
        row = lax.broadcasted_iota(jnp.int32, query.shape, 0)
        out[:, at] = jnp.where(row < alive[0], query, 0.0)


def mix_kernel(y, query, out):
    for i in range(out.shape[1] // 128):
        at = pl.ds(i * 128, 128)
        top, bottom = lane_mix(y[2 * i].astype(F32), y[2 * i + 1].astype(F32))
        out[:, at] = (query[:, at] * jnp.concatenate([top, bottom], axis=0)).astype(BF16)


def vmem(count):
    return [pl.BlockSpec(memory_space=pltpu.VMEM)] * count


def params(limit):
    return pltpu.CompilerParams(vmem_limit_bytes=limit * 1024 * 1024)


def per_device(rows, lengths, short_weight, long_filter, filter_bias):
    tok, width = rows.shape[1], rows.shape[3]
    nseq = lax.axis_size("seq")
    ngrp = lax.axis_size("grp")
    me = lax.axis_index("seq")
    chans = width // nseq
    half = tok // 2
    span = long_filter.shape[1]
    parts = jnp.transpose(rows[0], (1, 0, 2))
    alive = lengths - me * tok
    last, long_filter = lax.optimization_barrier((parts[:, tok - 2 :, :], long_filter))
    halo = lax.ppermute(last, "seq", [(i, i + 1) for i in range(nseq - 1)])
    mats, turns = [jnp.asarray(t) for t in transform_tables(nseq, tok)]

    own = pl.pallas_call(
        turn_filter_kernel,
        out_shape=jax.ShapeDtypeStruct((span // tok, half, 2 * chans), BF16),
        in_specs=vmem(1),
        out_specs=pl.BlockSpec(memory_space=pltpu.VMEM),
        compiler_params=params(24),
        name="turn_filter",
    )(long_filter)
    group = lax.axis_index("grp")

    def from_shift(x, shift):
        return lax.ppermute(x, "grp", [((i + shift) % ngrp, i) for i in range(ngrp)])

    two = jnp.concatenate([own, from_shift(own, 4)], axis=0)
    pair = parts[1:]
    block = 1024
    z = pl.pallas_call(
        gate_kernel,
        grid=(width // block,),
        out_shape=jax.ShapeDtypeStruct((nseq, half, 2 * chans), BF16),
        in_specs=[
            pl.BlockSpec(memory_space=pltpu.SMEM),
            pl.BlockSpec((2, tok, block), lambda i: (0, 0, i)),
            pl.BlockSpec((3, 2, block), lambda i: (0, 0, i)),
            pl.BlockSpec((2, 3, block), lambda i: (0, 0, i)),
        ],
        out_specs=pl.BlockSpec((block // chans, half, 2 * chans), lambda i: (i, 0, 0)),
        compiler_params=params(48),
        name="gate",
    )(alive, pair, halo, short_weight[1:])
    z, two = lax.optimization_barrier((z, two))
    across = [((i + (2 if i % 2 == 0 else 6)) % ngrp, i) for i in range(ngrp)]
    others = [lax.ppermute(two, "grp", across), from_shift(two, 1), from_shift(two, 7)]
    z = lax.all_to_all(z, "seq", split_axis=0, concat_axis=0, tiled=True)

    query = pl.pallas_call(
        query_kernel,
        grid=(width // block,),
        out_shape=jax.ShapeDtypeStruct((tok, width), F32),
        in_specs=[
            pl.BlockSpec(memory_space=pltpu.SMEM),
            pl.BlockSpec((1, tok, block), lambda i: (0, 0, i)),
            pl.BlockSpec((1, 2, block), lambda i: (0, 0, i)),
            pl.BlockSpec((1, 3, block), lambda i: (0, 0, i)),
        ],
        out_specs=pl.BlockSpec((tok, block), lambda i: (0, i)),
        compiler_params=params(48),
        cost_estimate=pl.CostEstimate(flops=2000000, bytes_accessed=2000000, transcendentals=0),
        name="query",
    )(alive, parts, halo, short_weight)

    hbm = pl.BlockSpec(memory_space=pltpu.HBM)
    table_scratch = [
        pltpu.VMEM((nseq // 2, 2 * tok, 2 * chans), BF16),
        pltpu.VMEM(mats.shape, BF16),
        pltpu.VMEM(turns.shape, F32),
    ]
    spec = pl.pallas_call(
        filter_kernel,
        out_shape=jax.ShapeDtypeStruct((nseq // 2, 2 * tok, 2 * chans), BF16),
        in_specs=[pl.BlockSpec(memory_space=pltpu.SMEM)] + vmem(5) + [hbm] * 2,
        out_specs=hbm,
        scratch_shapes=[
            pltpu.VMEM((nseq * (half + PAD), 128), F32),
            pltpu.VMEM((half * (2 * nseq + PAD), 128), F32),
            *table_scratch,
            pltpu.SemaphoreType.DMA((6,)),
        ],
        compiler_params=params(52),
        cost_estimate=pl.CostEstimate(flops=2000000000, bytes_accessed=6000000, transcendentals=0),
        name="filter_spectrum",
    )(group[None], two, *others, filter_bias[None], mats, turns)

    y = pl.pallas_call(
        conv_kernel,
        out_shape=jax.ShapeDtypeStruct((nseq, half, 2 * chans), BF16),
        in_specs=vmem(1) + [hbm] * 3,
        out_specs=pl.BlockSpec(memory_space=pltpu.VMEM),
        scratch_shapes=[
            pltpu.VMEM((nseq * (half + PAD), 128), F32),
            pltpu.VMEM((half * (2 * nseq + PAD), 128), F32),
            pltpu.VMEM((nseq // 2 * (2 * tok + PAD), 128), F32),
            *table_scratch,
            pltpu.SemaphoreType.DMA((6,)),
        ],
        compiler_params=params(52),
        name="convolve",
    )(z, spec, mats, turns)
    y = lax.all_to_all(y, "seq", split_axis=0, concat_axis=0, tiled=True)

    block = 1024
    out = pl.pallas_call(
        mix_kernel,
        grid=(width // block,),
        out_shape=jax.ShapeDtypeStruct((tok, width), BF16),
        in_specs=[
            pl.BlockSpec((block // chans, half, 2 * chans), lambda i: (i, 0, 0)),
            pl.BlockSpec((tok, block), lambda i: (0, i)),
        ],
        out_specs=pl.BlockSpec((tok, block), lambda i: (0, i)),
        compiler_params=params(24),
        name="mix",
    )(y, query)
    return out[None]


def solution(mesh):
    in_specs = (P("grp", "seq", None, None), P("grp"), P(), P("seq", "grp"), P("seq"))
    out_specs = P("grp", "seq", None)
    return jax.shard_map(
        per_device, mesh=mesh, in_specs=in_specs, out_specs=out_specs, check_vma=False
    )
```

time: 100 us -> 88 us (0.88)
  blocking collectives: 26.8 us -> 0 us
  starting transfers between devices: 28.8 us -> 47.8 us
  local copies, waits for them, and re-layouts: 9.84 us -> 3.28 us
  waiting for transfers between devices: 19.3 us -> 22.5 us
  Pallas kernels: 14.2 us -> 13.1 us
    all_gather x1 -> x0, blocking collectives: 26.8 us -> none  [per_device(): whole = lax.all_gather(own, 'grp', axis=0, tiled=True)]
    ppermute x1 -> x5, starting transfers between devices: 4.64 us -> 24.7 us  [the longest x3 18.9 us: from_shift(): lax.ppermute(x, 'grp', [((i + shift) % ngrp, i) for i in range(ngrp)])]
    unnamed x28 -> x14, local copies, waits for them, and re-layouts: 6.88 us -> 0.94 us
    all_to_all x1, starting transfers between devices: 15.1 us -> 11.7 us  [per_device(): y = lax.all_to_all(y, 'seq', split_axis=0, concat_axis=0, tiled=True)]
    ppermute x1 -> x5, waiting for transfers between devices: 2.22 us -> 5.28 us  [the longest x3 5.28 us: from_shift(): lax.ppermute(x, 'grp', [((i + shift) % ngrp, i) for i in range(ngrp)])]
    all_to_all x1, starting transfers between devices: 9.01 us -> 11.3 us  [per_device(): z = lax.all_to_all(z, 'seq', split_axis=0, concat_axis=0, tiled=True)]
    pallas_call x1, Pallas kernels: 6.5 us -> 5.25 us  [per_device(): pl.pallas_call(conv_kernel, out_shape=jax.ShapeDtypeStruct((nseq, half, 2...]
  transfers between devices with their start and end apart: 3 -> 7, of which waited for: 2 -> 4; matrix products, arithmetic and copies ran while one was open for 2% -> 2% of each run, Pallas kernels for 4% -> 7%
where the time goes in v1:
time: 88 us; the launch traced here: 87.5 us
  starting transfers between devices  47.8 us (54%)
  waiting for transfers between devices  22.5 us (26%)
  Pallas kernels  13.1 us (15%)
  local copies, waits for them, and re-layouts  3.28 us (4%)
    ppermute x3, starting transfers between devices, from_shift(): lax.ppermute(x, 'grp', [((i + shift) % ngrp, i) for i in range(ngrp)])  18.9 us
    all_to_all x1, waiting for transfers between devices, per_device(): y = lax.all_to_all(y, 'seq', split_axis=0, concat_axis=0, tiled=True)  17.1 us
    all_to_all x1, starting transfers between devices, per_device(): y = lax.all_to_all(y, 'seq', split_axis=0, concat_axis=0, tiled=True)  11.7 us
    all_to_all x1, starting transfers between devices, per_device(): z = lax.all_to_all(z, 'seq', split_axis=0, concat_axis=0, tiled=True)  11.3 us
    ppermute x3, waiting for transfers between devices, from_shift(): lax.ppermute(x, 'grp', [((i + shift) % ngrp, i) for i in range(ngrp)])  5.28 us
    pallas_call x1, Pallas kernels, per_device(): pl.pallas_call(conv_kernel, out_shape=jax.ShapeDtypeStruct((nseq, half, 2...  5.25 us
    ppermute x1, starting transfers between devices, per_device(): halo = lax.ppermute(last, 'seq', [(i, i + 1) for i in range(nseq - 1)])  3.96 us
    pallas_call x1, Pallas kernels, per_device(): pl.pallas_call(filter_kernel, out_shape=jax.ShapeDtypeStruct((nseq // 2,...  2.88 us
  transfers between devices with their start and end apart: 7, of which 4 were waited for; matrix products, arithmetic and copies ran while one was open for 2% of the time, Pallas kernels for 7%

profile of v1, /device:TPU:1, one launch (start us, length us, event | category | flops | bytes accessed | tf_op | source)
XLA Modules:
  0.0 87.5 jit_solution(9716596287853356264)
XLA Ops:
  0.0 0.0 copy-start.2
  0.0 1.0 %slice.13 = bf16[3,2,4096]{2,1,0:T(2,128)(2,1)S(1)} slice(bf16[3,64,4096]{2,1,0:T(8,128)(2,1)} %bitcast.7), slice={[0:3], [62:64], [0:4096]} | slice | bytes 98304 | tf_op jit(solution)/shard_map/slice | solution.py:278
  1.0 0.0 copy-start.5
  1.0 0.9 %copy-done.5 = f32[64,512]{1,0:T(8,128)S(1)} copy-done((f32[64,512]{1,0:T(8,128)S(1)}, f32[64,512]{1,0:T(8,128)}, u32[]{:S(2)}) %copy-start.5) | copy-done | bytes 131096
  1.9 0.2 turn_filter.1
  2.1 11.5 %collective-permute-start.1 = (bf16[8,32,128]{2,1,0:T(8,128)(2,1)S(1)}, bf16[8,32,128]{2,1,0:T(8,128)(2,1)S(1)}, u32[]{:S(2)}, u32[]{:S(2)}) collective-permute-start(bf16[8,32,128]{2,1,0:T(8,128)(2,1)S(1)} %turn_filter.1), channel_id=1, source_target_pairs={{256,0},{320,64},{384,128},{448,192},{0,256},{64,320},{128,384},{1... | collective-permute-start | bytes 196616 | tf_op jit(solution)/shard_map/ppermute | solution.py:293
  13.6 4.0 %collective-permute-start = (bf16[3,2,4096]{2,1,0:T(2,128)(2,1)S(1)}, bf16[3,2,4096]{2,1,0:T(2,128)(2,1)S(1)}, u32[]{:S(2)}, u32[]{:S(2)}) collective-permute-start(bf16[3,2,4096]{2,1,0:T(2,128)(2,1)S(1)} %slice.13), channel_id=1, source_target_pairs={{0,1},{1,2},{2,3},{3,4},{4,5},{5,6},{6,7},{7,8},{8,9},{9,10},{10,1... | collective-permute-start | bytes 147464 | tf_op jit(solution)/shard_map/ppermute | solution.py:279
  17.6 1.3 %slice.12.rows = bf16[2,64,4096]{2,1,0:T(8,128)(2,1)S(1)} slice(bf16[3,64,4096]{2,1,0:T(8,128)(2,1)} %bitcast.8), slice={[1:3], [0:64], [0:4096]} | slice | bytes 2097152 | tf_op jit(solution)/shard_map/slice | solution.py:296
  19.5 0.0 copy-done.2
  19.6 0.0 copy-start.1
  19.6 0.0 copy-start.3
  19.6 0.0 copy-start.6
  19.6 0.0 collective-permute-done.halo
  19.6 2.4 %gate.1 = bf16[64,32,128]{2,1,0:T(8,128)(2,1)} custom-call(s32[1]{0:T(128)S(6)} %sub.7.alive, bf16[2,64,4096]{2,1,0:T(8,128)(2,1)S(1)} %slice.12.rows, bf16[3,2,4096]{2,1,0:T(2,128)(2,1)S(1)} %collective-permute-done.halo, f32[2,3,4096]{2,1,0:T(4,128)S(1)} %slice.11.weights), custom_call_target="tpu_custom_call" | custom-call | tf_op jit(solution)/shard_map/gate/pallas_call | solution.py:298
  22.0 0.0 collective-permute-done.1
  22.0 11.3 %all-to-all-start = ((bf16[64,32,128]{2,1,0:T(8,128)(2,1)}), bf16[64,32,128]{2,1,0:T(8,128)(2,1)S(1)}, u32[]{:S(2)}, u32[]{:S(2)}) async-start(bf16[64,32,128]{2,1,0:T(8,128)(2,1)} %gate.1), calls=%async_computation | async-start | bytes 1048576 | tf_op jit(solution)/shard_map/all_to_all | solution.py:315
  33.3 1.9 %collective-permute-start.2 = (bf16[16,32,128]{2,1,0:T(8,128)(2,1)S(1)}, bf16[16,32,128]{2,1,0:T(8,128)(2,1)S(1)}, u32[]{:S(2)}, u32[]{:S(2)}) collective-permute-start(bf16[16,32,128]{2,1,0:T(8,128)(2,1)S(1)} %pad_maximum_fusion.own), channel_id=1, source_target_pairs={{128,0},{448,64},{256,128},{64,192},{384,256},{192,320},{0,384},{3... | collective-permute-start | bytes 393224 | tf_op jit(solution)/shard_map/ppermute | solution.py:314
  35.3 5.5 %collective-permute-start.3 = (bf16[16,32,128]{2,1,0:T(8,128)(2,1)S(1)}, bf16[16,32,128]{2,1,0:T(8,128)(2,1)S(1)}, u32[]{:S(2)}, u32[]{:S(2)}) collective-permute-start(bf16[16,32,128]{2,1,0:T(8,128)(2,1)S(1)} %pad_maximum_fusion.own), channel_id=1, source_target_pairs={{64,0},{128,64},{192,128},{256,192},{320,256},{384,320},{448,384},... | collective-permute-start | bytes 393224 | tf_op jit(solution)/shard_map/ppermute | solution.py:293
  40.8 1.9 %collective-permute-start.4 = (bf16[16,32,128]{2,1,0:T(8,128)(2,1)S(1)}, bf16[16,32,128]{2,1,0:T(8,128)(2,1)S(1)}, u32[]{:S(2)}, u32[]{:S(2)}) collective-permute-start(bf16[16,32,128]{2,1,0:T(8,128)(2,1)S(1)} %pad_maximum_fusion.own), channel_id=1, source_target_pairs={{448,0},{0,64},{64,128},{128,192},{192,256},{256,320},{320,384},{3... | collective-permute-start | bytes 393224 | tf_op jit(solution)/shard_map/ppermute | solution.py:293
  42.7 0.0 collective-permute-done.2.across
  42.7 0.9 %collective-permute-done.3.one_on = bf16[16,32,128]{2,1,0:T(8,128)(2,1)S(1)} collective-permute-done((bf16[16,32,128]{2,1,0:T(8,128)(2,1)S(1)}, bf16[16,32,128]{2,1,0:T(8,128)(2,1)S(1)}, u32[]{:S(2)}, u32[]{:S(2)}) %collective-permute-start.3) | collective-permute-done | bytes 131104 | tf_op jit(solution)/shard_map/ppermute | solution.py:293
  43.6 4.4 %collective-permute-done.4.one_back = bf16[16,32,128]{2,1,0:T(8,128)(2,1)S(1)} collective-permute-done((bf16[16,32,128]{2,1,0:T(8,128)(2,1)S(1)}, bf16[16,32,128]{2,1,0:T(8,128)(2,1)S(1)}, u32[]{:S(2)}, u32[]{:S(2)}) %collective-permute-start.4) | collective-permute-done | bytes 131104 | tf_op jit(solution)/shard_map/ppermute | solution.py:293
  48.0 0.0 copy-done.1
  48.0 0.0 copy-done.3
  48.0 0.0 copy-done.6
  48.0 0.0 copy-start.4
  48.0 2.9 %filter_spectrum.1.spec_in = bf16[32,128,128]{2,1,0:T(8,128)(2,1)} custom-call(s32[1]{0:T(128)} %bitcast.4.place, bf16[16,32,128]{2,1,0:T(8,128)(2,1)S(1)} %pad_maximum_fusion.own, bf16[16,32,128]{2,1,0:T(8,128)(2,1)S(1)} %collective-permute-done.2.across, bf16[16,32,128]{2,1,0:T(8,128)(2,1)S(1)} %collective-permute-done.3.one_on, ...), custom_call_target="tpu_custom_call" | custom-call | flops 2000000000 | bytes 6000000 | tf_op jit(solution)/shard_map/filter_spectrum/pallas_call | solution.py:339
  50.9 0.0 copy-start
  50.9 0.2 all-to-all-done.z
  51.1 0.0 copy-done.4
  51.1 5.2 %convolve.1 = bf16[64,32,128]{2,1,0:T(8,128)(2,1)} custom-call(bf16[64,32,128]{2,1,0:T(8,128)(2,1)S(1)} %all-to-all-done.z, bf16[32,128,128]{2,1,0:T(8,128)(2,1)} %filter_spectrum.1.spec_in, bf16[448,256]{1,0:T(8,128)(2,1)S(1)} %copy-done.4, f32[2,12,64,128]{3,2,1,0:T(8,128)} %constant.16.clone.turns_in), custom_call_target="tpu_custom_call" | custom-call | tf_op jit(solution)/shard_map/convolve/pallas_call | solution.py:355
  56.3 11.7 %all-to-all-start.1 = ((bf16[64,32,128]{2,1,0:T(8,128)(2,1)}), bf16[64,32,128]{2,1,0:T(8,128)(2,1)S(1)}, u32[]{:S(2)}, u32[]{:S(2)}) async-start(bf16[64,32,128]{2,1,0:T(8,128)(2,1)} %convolve.1), calls=%async_computation.1 | async-start | bytes 1048576 | tf_op jit(solution)/shard_map/all_to_all | solution.py:370
  68.1 0.0 copy-done
  68.1 0.6 query.1
  68.7 17.1 %all-to-all-done.1.y = bf16[64,32,128]{2,1,0:T(8,128)(2,1)S(1)} async-done(((bf16[64,32,128]{2,1,0:T(8,128)(2,1)}), bf16[64,32,128]{2,1,0:T(8,128)(2,1)S(1)}, u32[]{:S(2)}, u32[]{:S(2)}) %all-to-all-start.1) | async-done | bytes 524320 | tf_op jit(solution)/shard_map/all_to_all | solution.py:370
  85.8 1.8 %mix.1 = bf16[64,4096]{1,0:T(8,128)(2,1)} custom-call(bf16[64,32,128]{2,1,0:T(8,128)(2,1)S(1)} %all-to-all-done.1.y, f32[64,4096]{1,0:T(8,128)S(1)} %query.1), custom_call_target="tpu_custom_call" | custom-call | tf_op jit(solution)/shard_map/mix/pallas_call | solution.py:373
  (2 shorter events, 0.0 us)
Async XLA Ops:
  0.0 19.5 %copy-start.2 = (f32[3,3,4096]{2,1,0:T(4,128)S(1)}, f32[3,3,4096]{2,1,0:T(4,128)}, u32[]{:S(2)}) copy-start(f32[3,3,4096]{2,1,0:T(4,128)} %weights.1) | copy-start | bytes 442372
  1.0 0.9 %copy-start.5 = (f32[64,512]{1,0:T(8,128)S(1)}, f32[64,512]{1,0:T(8,128)}, u32[]{:S(2)}) copy-start(f32[64,512]{1,0:T(8,128)} %filt) | copy-start | bytes 393220
  2.1 19.8 %collective-permute-start.1 = (bf16[8,32,128]{2,1,0:T(8,128)(2,1)S(1)}, bf16[8,32,128]{2,1,0:T(8,128)(2,1)S(1)}, u32[]{:S(2)}, u32[]{:S(2)}) collective-permute-start(bf16[8,32,128]{2,1,0:T(8,128)(2,1)S(1)} %turn_filter.1), channel_id=1, source_target_pairs={{256,0},{320,64},{384,128},{448,192},{0,256},{64,320},{128,384},{1... | collective-permute-start | bytes 196616 | tf_op jit(solution)/shard_map/ppermute | solution.py:293
  13.6 6.0 %collective-permute-start = (bf16[3,2,4096]{2,1,0:T(2,128)(2,1)S(1)}, bf16[3,2,4096]{2,1,0:T(2,128)(2,1)S(1)}, u32[]{:S(2)}, u32[]{:S(2)}) collective-permute-start(bf16[3,2,4096]{2,1,0:T(2,128)(2,1)S(1)} %slice.13), channel_id=1, source_target_pairs={{0,1},{1,2},{2,3},{3,4},{4,5},{5,6},{6,7},{7,8},{8,9},{9,10},{10,1... | collective-permute-start | bytes 147464 | tf_op jit(solution)/shard_map/ppermute | solution.py:279
  19.6 28.4 %copy-start.1 = (f32[2,12,64,128]{3,2,1,0:T(8,128)S(1)}, f32[2,12,64,128]{3,2,1,0:T(8,128)}, u32[]{:S(2)}) copy-start(f32[2,12,64,128]{3,2,1,0:T(8,128)} %constant.16.clone.turns_in) | copy-start | bytes 2359300
  19.6 28.4 %copy-start.3 = (bf16[448,256]{1,0:T(8,128)(2,1)S(1)}, bf16[448,256]{1,0:T(8,128)(2,1)}, u32[]{:S(2)}) copy-start(bf16[448,256]{1,0:T(8,128)(2,1)} %constant.15.clone.mats_in) | copy-start | bytes 688132
  19.6 28.4 %copy-start.6 = (f32[64]{0:T(128)S(1)}, f32[64]{0:T(128)}, u32[]{:S(2)}) copy-start(f32[64]{0:T(128)} %param.11) | copy-start | bytes 772
  22.0 29.0 %all-to-all-start = ((bf16[64,32,128]{2,1,0:T(8,128)(2,1)}), bf16[64,32,128]{2,1,0:T(8,128)(2,1)S(1)}, u32[]{:S(2)}, u32[]{:S(2)}) async-start(bf16[64,32,128]{2,1,0:T(8,128)(2,1)} %gate.1), calls=%async_computation | async-start | bytes 1048576 | tf_op jit(solution)/shard_map/all_to_all | solution.py:315
  33.3 9.4 %collective-permute-start.2 = (bf16[16,32,128]{2,1,0:T(8,128)(2,1)S(1)}, bf16[16,32,128]{2,1,0:T(8,128)(2,1)S(1)}, u32[]{:S(2)}, u32[]{:S(2)}) collective-permute-start(bf16[16,32,128]{2,1,0:T(8,128)(2,1)S(1)} %pad_maximum_fusion.own), channel_id=1, source_target_pairs={{128,0},{448,64},{256,128},{64,192},{384,256},{192,320},{0,384},{3... | collective-permute-start | bytes 393224 | tf_op jit(solution)/shard_map/ppermute | solution.py:314
  35.3 8.3 %collective-permute-start.3 = (bf16[16,32,128]{2,1,0:T(8,128)(2,1)S(1)}, bf16[16,32,128]{2,1,0:T(8,128)(2,1)S(1)}, u32[]{:S(2)}, u32[]{:S(2)}) collective-permute-start(bf16[16,32,128]{2,1,0:T(8,128)(2,1)S(1)} %pad_maximum_fusion.own), channel_id=1, source_target_pairs={{64,0},{128,64},{192,128},{256,192},{320,256},{384,320},{448,384},... | collective-permute-start | bytes 393224 | tf_op jit(solution)/shard_map/ppermute | solution.py:293
  40.8 7.2 %collective-permute-start.4 = (bf16[16,32,128]{2,1,0:T(8,128)(2,1)S(1)}, bf16[16,32,128]{2,1,0:T(8,128)(2,1)S(1)}, u32[]{:S(2)}, u32[]{:S(2)}) collective-permute-start(bf16[16,32,128]{2,1,0:T(8,128)(2,1)S(1)} %pad_maximum_fusion.own), channel_id=1, source_target_pairs={{448,0},{0,64},{64,128},{128,192},{192,256},{256,320},{320,384},{3... | collective-permute-start | bytes 393224 | tf_op jit(solution)/shard_map/ppermute | solution.py:293
  48.0 3.1 %copy-start.4 = (bf16[448,256]{1,0:T(8,128)(2,1)S(1)}, bf16[448,256]{1,0:T(8,128)(2,1)}, u32[]{:S(2)}) copy-start(bf16[448,256]{1,0:T(8,128)(2,1)} %constant.15.clone.mats_in) | copy-start | bytes 688132
  50.9 17.2 %copy-start = (bf16[1,64,3,4096]{3,1,2,0:T(8,128)(2,1)S(1)}, bf16[1,64,3,4096]{3,1,2,0:T(8,128)(2,1)}, u32[]{:S(2)}) copy-start(bf16[1,64,3,4096]{3,1,2,0:T(8,128)(2,1)} %param.7) | copy-start | bytes 4718596
  56.3 29.5 %all-to-all-start.1 = ((bf16[64,32,128]{2,1,0:T(8,128)(2,1)}), bf16[64,32,128]{2,1,0:T(8,128)(2,1)S(1)}, u32[]{:S(2)}, u32[]{:S(2)}) async-start(bf16[64,32,128]{2,1,0:T(8,128)(2,1)} %convolve.1), calls=%async_computation.1 | async-start | bytes 1048576 | tf_op jit(solution)/shard_map/all_to_all | solution.py:370

commit v2 on v1

--- a/solution.py
+++ b/solution.py
@@ -159,7 +159,7 @@
         leave.wait()
 
 
-def conv_kernel(z, spec_in, mats_in, turns_in, out, data32, mid, mid_back, spec, mats, turns, sems):
+def conv_kernel(z, spec_in, mats_in, turns_in, out, held, data32, mid, mid_back, spec, mats, turns, sems):
     na, nr, _ = z.shape
     nb = 2 * nr
     step = na // 8
@@ -206,8 +206,14 @@
         got = dot(first_back, twice(jnp.concatenate(cols, axis=1)))
         for j, s in enumerate((r, r + 1)):
             data32[pl.ds(s, na, stride=nr + PAD), :] = got[:, j * 128 : (j + 1) * 128]
+    made = []
     for a in range(na):
-        out[a] = data32[pl.ds(a * (nr + PAD), nr), :].astype(BF16)
+        held[a] = data32[pl.ds(a * (nr + PAD), nr), :].astype(BF16)
+        if (a + 1) % (na // 4) == 0:
+            part = pl.ds(a + 1 - na // 4, na // 4)
+            made += copies([(held.at[part], out.at[part])], sems.at[pl.ds(a // (na // 4), 1)])
+    for copy in made:
+        copy.wait()
 
 
 def turn_filter_kernel(filt, out):
@@ -230,16 +236,24 @@
     return weights[0:1] * x + weights[1:2] * back1 + weights[2:3] * back2
 
 
-def gate_kernel(alive, rows, halo, weights, out):
-    for i in range(rows.shape[2] // 128):
+def gate_kernel(alive, rows, halo, weights, out, held, sems):
+    count = rows.shape[2] // 128
+    step = count // 4
+    made = []
+    for i in range(count):
         at = pl.ds(i * 128, 128)
         key = short_sum(rows[0, :, at], halo[1, :, at], weights[0, :, at], alive[0])
         val = short_sum(rows[1, :, at], halo[2, :, at], weights[1, :, at], alive[0])
         z = key * val
         half = z.shape[0] // 2
         one, two = lane_mix(z[:half], z[half:])
-        out[2 * i] = one.astype(BF16)
-        out[2 * i + 1] = two.astype(BF16)
+        held[2 * i] = one.astype(BF16)
+        held[2 * i + 1] = two.astype(BF16)
+        if (i + 1) % step == 0:
+            part = pl.ds(2 * (i + 1 - step), 2 * step)
+            made += copies([(held.at[part], out.at[part])], sems.at[pl.ds(i // step, 1)])
+    for copy in made:
+        copy.wait()
 
 
 def query_kernel(alive, rows, halo, weights, out):
@@ -250,11 +264,19 @@
         out[:, at] = jnp.where(row < alive[0], query, 0.0)
 
 
-def mix_kernel(y, query, out):
-    for i in range(out.shape[1] // 128):
+def mix_kernel(y, query, out, held, sems):
+    count = out.shape[1] // 128
+    step = count // 4
+    made = []
+    for i in range(count):
         at = pl.ds(i * 128, 128)
         top, bottom = lane_mix(y[2 * i].astype(F32), y[2 * i + 1].astype(F32))
-        out[:, at] = (query[:, at] * jnp.concatenate([top, bottom], axis=0)).astype(BF16)
+        held[:, at] = (query[:, at] * jnp.concatenate([top, bottom], axis=0)).astype(BF16)
+        if (i + 1) % step == 0:
+            part = pl.ds((i + 1 - step) * 128, step * 128)
+            made += copies([(held.at[:, part], out.at[:, part])], sems.at[pl.ds(i // step, 1)])
+    for copy in made:
+        copy.wait()
 
 
 def vmem(count):
@@ -294,19 +316,19 @@
 
     two = jnp.concatenate([own, from_shift(own, 4)], axis=0)
     pair = parts[1:]
+    hbm = pl.BlockSpec(memory_space=pltpu.HBM)
     block = 1024
     z = pl.pallas_call(
         gate_kernel,
-        grid=(width // block,),
         out_shape=jax.ShapeDtypeStruct((nseq, half, 2 * chans), BF16),
-        in_specs=[
-            pl.BlockSpec(memory_space=pltpu.SMEM),
-            pl.BlockSpec((2, tok, block), lambda i: (0, 0, i)),
-            pl.BlockSpec((3, 2, block), lambda i: (0, 0, i)),
-            pl.BlockSpec((2, 3, block), lambda i: (0, 0, i)),
+        in_specs=[pl.BlockSpec(memory_space=pltpu.SMEM)] + vmem(3),
+        out_specs=hbm,
+        scratch_shapes=[
+            pltpu.VMEM((nseq, half, 2 * chans), BF16),
+            pltpu.SemaphoreType.DMA((4,)),
         ],
-        out_specs=pl.BlockSpec((block // chans, half, 2 * chans), lambda i: (i, 0, 0)),
         compiler_params=params(48),
+        cost_estimate=pl.CostEstimate(flops=1000000000, bytes_accessed=2000000, transcendentals=0),
         name="gate",
     )(alive, pair, halo, short_weight[1:])
     z, two = lax.optimization_barrier((z, two))
@@ -330,7 +352,6 @@
         name="query",
     )(alive, parts, halo, short_weight)
 
-    hbm = pl.BlockSpec(memory_space=pltpu.HBM)
     table_scratch = [
         pltpu.VMEM((nseq // 2, 2 * tok, 2 * chans), BF16),
         pltpu.VMEM(mats.shape, BF16),
@@ -356,8 +377,9 @@
         conv_kernel,
         out_shape=jax.ShapeDtypeStruct((nseq, half, 2 * chans), BF16),
         in_specs=vmem(1) + [hbm] * 3,
-        out_specs=pl.BlockSpec(memory_space=pltpu.VMEM),
+        out_specs=hbm,
         scratch_shapes=[
+            pltpu.VMEM((nseq, half, 2 * chans), BF16),
             pltpu.VMEM((nseq * (half + PAD), 128), F32),
             pltpu.VMEM((half * (2 * nseq + PAD), 128), F32),
             pltpu.VMEM((nseq // 2 * (2 * tok + PAD), 128), F32),
@@ -369,16 +391,15 @@
     )(z, spec, mats, turns)
     y = lax.all_to_all(y, "seq", split_axis=0, concat_axis=0, tiled=True)
 
-    block = 1024
     out = pl.pallas_call(
         mix_kernel,
-        grid=(width // block,),
         out_shape=jax.ShapeDtypeStruct((tok, width), BF16),
-        in_specs=[
-            pl.BlockSpec((block // chans, half, 2 * chans), lambda i: (i, 0, 0)),
-            pl.BlockSpec((tok, block), lambda i: (0, i)),
+        in_specs=vmem(2),
+        out_specs=hbm,
+        scratch_shapes=[
+            pltpu.VMEM((tok, width), BF16),
+            pltpu.SemaphoreType.DMA((4,)),
         ],
-        out_specs=pl.BlockSpec((tok, block), lambda i: (0, i)),
         compiler_params=params(24),
         name="mix",
     )(y, query)

time: 88 us -> 86.4 us (0.982)
  Pallas kernels: 13.1 us -> 11.7 us
  waiting for transfers between devices: 22.5 us -> 21.1 us
  starting transfers between devices: 47.8 us -> 48.9 us
    ppermute x1, starting transfers between devices: 1.92 us -> 6.97 us  [per_device(): lax.ppermute(two, 'grp', across)]
    ppermute x3, starting transfers between devices: 18.9 us -> 15.9 us  [from_shift(): lax.ppermute(x, 'grp', [((i + shift) % ngrp, i) for i in range(ngrp)])]
    pallas_call x2, Pallas kernels: 4.11 us -> 2.67 us  [the longest x1 1.72 us: per_device(): pl.pallas_call(gate_kernel, out_shape=jax.ShapeDtypeStruct((nseq, half, 2...]
    all_to_all x1, starting transfers between devices: 11.3 us -> 9.95 us  [per_device(): z = lax.all_to_all(z, 'seq', split_axis=0, concat_axis=0, tiled=True)]
    ppermute x3, waiting for transfers between devices: 5.28 us -> 4.02 us  [from_shift(): lax.ppermute(x, 'grp', [((i + shift) % ngrp, i) for i in range(ngrp)])]
  transfers between devices with their start and end apart: 7 -> 7, of which waited for: 4 -> 3; matrix products, arithmetic and copies ran while one was open for 2% -> 2% of each run, Pallas kernels for 7% -> 6%
where the time goes in v2:
time: 86.4 us; the launch traced here: 85.9 us
  starting transfers between devices  48.9 us (57%)
  waiting for transfers between devices  21.1 us (24%)
  Pallas kernels  11.7 us (14%)
  local copies, waits for them, and re-layouts  3.28 us (4%)
  between operations  0.89 us (1%)
    all_to_all x1, waiting for transfers between devices, per_device(): y = lax.all_to_all(y, 'seq', split_axis=0, concat_axis=0, tiled=True)  17.1 us
    ppermute x3, starting transfers between devices, from_shift(): lax.ppermute(x, 'grp', [((i + shift) % ngrp, i) for i in range(ngrp)])  15.9 us
    all_to_all x1, starting transfers between devices, per_device(): y = lax.all_to_all(y, 'seq', split_axis=0, concat_axis=0, tiled=True)  11.6 us
    all_to_all x1, starting transfers between devices, per_device(): z = lax.all_to_all(z, 'seq', split_axis=0, concat_axis=0, tiled=True)  9.95 us
    ppermute x1, starting transfers between devices, per_device(): lax.ppermute(two, 'grp', across)  6.97 us
    pallas_call x1, Pallas kernels, per_device(): pl.pallas_call(conv_kernel, out_shape=jax.ShapeDtypeStruct((nseq, half, 2...  5.34 us
    ppermute x1, starting transfers between devices, per_device(): halo = lax.ppermute(last, 'seq', [(i, i + 1) for i in range(nseq - 1)])  4.51 us
    ppermute x3, waiting for transfers between devices, from_shift(): lax.ppermute(x, 'grp', [((i + shift) % ngrp, i) for i in range(ngrp)])  4.02 us
  transfers between devices with their start and end apart: 7, of which 3 were waited for; matrix products, arithmetic and copies ran while one was open for 2% of the time, Pallas kernels for 6%

profile of v2, /device:TPU:1, one launch (start us, length us, event | category | flops | bytes accessed | tf_op | source)
XLA Modules:
  0.0 85.9 jit_solution(6795570911511267730)
XLA Ops:
  0.0 0.0 copy-start.2
  0.0 1.0 %slice.13 = bf16[3,2,4096]{2,1,0:T(2,128)(2,1)S(1)} slice(bf16[3,64,4096]{2,1,0:T(8,128)(2,1)} %bitcast.7), slice={[0:3], [62:64], [0:4096]} | slice | bytes 98304 | tf_op jit(solution)/shard_map/slice | solution.py:300
  1.0 4.5 %collective-permute-start = (bf16[3,2,4096]{2,1,0:T(2,128)(2,1)S(1)}, bf16[3,2,4096]{2,1,0:T(2,128)(2,1)S(1)}, u32[]{:S(2)}, u32[]{:S(2)}) collective-permute-start(bf16[3,2,4096]{2,1,0:T(2,128)(2,1)S(1)} %slice.13), channel_id=1, source_target_pairs={{0,1},{1,2},{2,3},{3,4},{4,5},{5,6},{6,7},{7,8},{8,9},{9,10},{10,1... | collective-permute-start | bytes 147464 | tf_op jit(solution)/shard_map/ppermute | solution.py:301
  5.5 0.0 copy-start.5
  5.6 0.9 %copy-done.5 = f32[64,512]{1,0:T(8,128)S(1)} copy-done((f32[64,512]{1,0:T(8,128)S(1)}, f32[64,512]{1,0:T(8,128)}, u32[]{:S(2)}) %copy-start.5) | copy-done | bytes 131096
  6.5 0.2 turn_filter.1
  6.7 10.6 %collective-permute-start.1 = (bf16[8,32,128]{2,1,0:T(8,128)(2,1)S(1)}, bf16[8,32,128]{2,1,0:T(8,128)(2,1)S(1)}, u32[]{:S(2)}, u32[]{:S(2)}) collective-permute-start(bf16[8,32,128]{2,1,0:T(8,128)(2,1)S(1)} %turn_filter.1), channel_id=1, source_target_pairs={{256,0},{320,64},{384,128},{448,192},{0,256},{64,320},{128,384},{1... | collective-permute-start | bytes 196616 | tf_op jit(solution)/shard_map/ppermute | solution.py:315
  17.3 1.3 %slice.12.rows = bf16[2,64,4096]{2,1,0:T(8,128)(2,1)S(1)} slice(bf16[3,64,4096]{2,1,0:T(8,128)(2,1)} %bitcast.8), slice={[1:3], [0:64], [0:4096]} | slice | bytes 2097152 | tf_op jit(solution)/shard_map/slice | solution.py:318
  19.3 0.0 copy-done.2
  19.3 0.0 copy-start.1
  19.3 0.0 copy-start.3
  19.3 0.0 copy-start.6
  19.4 0.0 collective-permute-done.halo
  19.4 1.7 %gate.1 = bf16[64,32,128]{2,1,0:T(8,128)(2,1)} custom-call(s32[1]{0:T(128)S(6)} %sub.7.alive, bf16[2,64,4096]{2,1,0:T(8,128)(2,1)S(1)} %slice.12.rows, bf16[3,2,4096]{2,1,0:T(2,128)(2,1)S(1)} %collective-permute-done.halo, f32[2,3,4096]{2,1,0:T(4,128)S(1)} %slice.11.weights), custom_call_target="tpu_custom_call" | custom-call | flops 1000000000 | bytes 2000000 | tf_op jit(solution)/shard_map/gate/pallas_call | solution.py:321
  21.1 0.0 collective-permute-done.1
  21.1 9.9 %all-to-all-start = ((bf16[64,32,128]{2,1,0:T(8,128)(2,1)}), bf16[64,32,128]{2,1,0:T(8,128)(2,1)S(1)}, u32[]{:S(2)}, u32[]{:S(2)}) async-start(bf16[64,32,128]{2,1,0:T(8,128)(2,1)} %gate.1), calls=%async_computation | async-start | bytes 1048576 | tf_op jit(solution)/shard_map/all_to_all | solution.py:337
  31.1 7.0 %collective-permute-start.2 = (bf16[16,32,128]{2,1,0:T(8,128)(2,1)S(1)}, bf16[16,32,128]{2,1,0:T(8,128)(2,1)S(1)}, u32[]{:S(2)}, u32[]{:S(2)}) collective-permute-start(bf16[16,32,128]{2,1,0:T(8,128)(2,1)S(1)} %pad_maximum_fusion.own), channel_id=1, source_target_pairs={{128,0},{448,64},{256,128},{64,192},{384,256},{192,320},{0,384},{3... | collective-permute-start | bytes 393224 | tf_op jit(solution)/shard_map/ppermute | solution.py:336
  38.0 1.9 %collective-permute-start.3 = (bf16[16,32,128]{2,1,0:T(8,128)(2,1)S(1)}, bf16[16,32,128]{2,1,0:T(8,128)(2,1)S(1)}, u32[]{:S(2)}, u32[]{:S(2)}) collective-permute-start(bf16[16,32,128]{2,1,0:T(8,128)(2,1)S(1)} %pad_maximum_fusion.own), channel_id=1, source_target_pairs={{64,0},{128,64},{192,128},{256,192},{320,256},{384,320},{448,384},... | collective-permute-start | bytes 393224 | tf_op jit(solution)/shard_map/ppermute | solution.py:315
  40.0 3.4 %collective-permute-start.4 = (bf16[16,32,128]{2,1,0:T(8,128)(2,1)S(1)}, bf16[16,32,128]{2,1,0:T(8,128)(2,1)S(1)}, u32[]{:S(2)}, u32[]{:S(2)}) collective-permute-start(bf16[16,32,128]{2,1,0:T(8,128)(2,1)S(1)} %pad_maximum_fusion.own), channel_id=1, source_target_pairs={{448,0},{0,64},{64,128},{128,192},{192,256},{256,320},{320,384},{3... | collective-permute-start | bytes 393224 | tf_op jit(solution)/shard_map/ppermute | solution.py:315
  43.4 0.0 collective-permute-done.2.across
  43.4 0.9 %collective-permute-done.3.one_on = bf16[16,32,128]{2,1,0:T(8,128)(2,1)S(1)} collective-permute-done((bf16[16,32,128]{2,1,0:T(8,128)(2,1)S(1)}, bf16[16,32,128]{2,1,0:T(8,128)(2,1)S(1)}, u32[]{:S(2)}, u32[]{:S(2)}) %collective-permute-start.3) | collective-permute-done | bytes 131104 | tf_op jit(solution)/shard_map/ppermute | solution.py:315
  44.2 3.1 %collective-permute-done.4.one_back = bf16[16,32,128]{2,1,0:T(8,128)(2,1)S(1)} collective-permute-done((bf16[16,32,128]{2,1,0:T(8,128)(2,1)S(1)}, bf16[16,32,128]{2,1,0:T(8,128)(2,1)S(1)}, u32[]{:S(2)}, u32[]{:S(2)}) %collective-permute-start.4) | collective-permute-done | bytes 131104 | tf_op jit(solution)/shard_map/ppermute | solution.py:315
  47.4 0.0 copy-done.1
  47.4 0.0 copy-done.3
  47.4 0.0 copy-done.6
  47.4 0.0 copy-start.4
  47.4 2.9 %filter_spectrum.1.spec_in = bf16[32,128,128]{2,1,0:T(8,128)(2,1)} custom-call(s32[1]{0:T(128)} %bitcast.4.place, bf16[16,32,128]{2,1,0:T(8,128)(2,1)S(1)} %pad_maximum_fusion.own, bf16[16,32,128]{2,1,0:T(8,128)(2,1)S(1)} %collective-permute-done.2.across, bf16[16,32,128]{2,1,0:T(8,128)(2,1)S(1)} %collective-permute-done.3.one_on, ...), custom_call_target="tpu_custom_call" | custom-call | flops 2000000000 | bytes 6000000 | tf_op jit(solution)/shard_map/filter_spectrum/pallas_call | solution.py:360
  50.3 0.0 copy-start
  50.3 0.0 all-to-all-done.z
  50.3 0.0 copy-done.4
  50.3 5.3 %convolve.1 = bf16[64,32,128]{2,1,0:T(8,128)(2,1)} custom-call(bf16[64,32,128]{2,1,0:T(8,128)(2,1)S(1)} %all-to-all-done.z, bf16[32,128,128]{2,1,0:T(8,128)(2,1)} %filter_spectrum.1.spec_in, bf16[448,256]{1,0:T(8,128)(2,1)S(1)} %copy-done.4, f32[2,12,64,128]{3,2,1,0:T(8,128)} %constant.16.clone.turns_in), custom_call_target="tpu_custom_call" | custom-call | tf_op jit(solution)/shard_map/convolve/pallas_call | solution.py:376
  55.7 11.6 %all-to-all-start.1 = ((bf16[64,32,128]{2,1,0:T(8,128)(2,1)}), bf16[64,32,128]{2,1,0:T(8,128)(2,1)S(1)}, u32[]{:S(2)}, u32[]{:S(2)}) async-start(bf16[64,32,128]{2,1,0:T(8,128)(2,1)} %convolve.1), calls=%async_computation.1 | async-start | bytes 1048576 | tf_op jit(solution)/shard_map/all_to_all | solution.py:392
  67.2 0.0 copy-done
  67.2 0.6 query.1
  67.9 17.1 %all-to-all-done.1.y = bf16[64,32,128]{2,1,0:T(8,128)(2,1)S(1)} async-done(((bf16[64,32,128]{2,1,0:T(8,128)(2,1)}), bf16[64,32,128]{2,1,0:T(8,128)(2,1)S(1)}, u32[]{:S(2)}, u32[]{:S(2)}) %all-to-all-start.1) | async-done | bytes 524320 | tf_op jit(solution)/shard_map/all_to_all | solution.py:392
  85.0 1.0 %mix.1 = bf16[64,4096]{1,0:T(8,128)(2,1)} custom-call(bf16[64,32,128]{2,1,0:T(8,128)(2,1)S(1)} %all-to-all-done.1.y, f32[64,4096]{1,0:T(8,128)S(1)} %query.1), custom_call_target="tpu_custom_call" | custom-call | tf_op jit(solution)/shard_map/mix/pallas_call | solution.py:394
  (2 shorter events, 0.0 us)
Async XLA Ops:
  0.0 19.3 %copy-start.2 = (f32[3,3,4096]{2,1,0:T(4,128)S(1)}, f32[3,3,4096]{2,1,0:T(4,128)}, u32[]{:S(2)}) copy-start(f32[3,3,4096]{2,1,0:T(4,128)} %weights.1) | copy-start | bytes 442372
  1.0 18.3 %collective-permute-start = (bf16[3,2,4096]{2,1,0:T(2,128)(2,1)S(1)}, bf16[3,2,4096]{2,1,0:T(2,128)(2,1)S(1)}, u32[]{:S(2)}, u32[]{:S(2)}) collective-permute-start(bf16[3,2,4096]{2,1,0:T(2,128)(2,1)S(1)} %slice.13), channel_id=1, source_target_pairs={{0,1},{1,2},{2,3},{3,4},{4,5},{5,6},{6,7},{7,8},{8,9},{9,10},{10,1... | collective-permute-start | bytes 147464 | tf_op jit(solution)/shard_map/ppermute | solution.py:301
  5.5 0.9 %copy-start.5 = (f32[64,512]{1,0:T(8,128)S(1)}, f32[64,512]{1,0:T(8,128)}, u32[]{:S(2)}) copy-start(f32[64,512]{1,0:T(8,128)} %filt) | copy-start | bytes 393220
  6.7 14.4 %collective-permute-start.1 = (bf16[8,32,128]{2,1,0:T(8,128)(2,1)S(1)}, bf16[8,32,128]{2,1,0:T(8,128)(2,1)S(1)}, u32[]{:S(2)}, u32[]{:S(2)}) collective-permute-start(bf16[8,32,128]{2,1,0:T(8,128)(2,1)S(1)} %turn_filter.1), channel_id=1, source_target_pairs={{256,0},{320,64},{384,128},{448,192},{0,256},{64,320},{128,384},{1... | collective-permute-start | bytes 196616 | tf_op jit(solution)/shard_map/ppermute | solution.py:315
  19.3 28.1 %copy-start.1 = (f32[2,12,64,128]{3,2,1,0:T(8,128)S(1)}, f32[2,12,64,128]{3,2,1,0:T(8,128)}, u32[]{:S(2)}) copy-start(f32[2,12,64,128]{3,2,1,0:T(8,128)} %constant.16.clone.turns_in) | copy-start | bytes 2359300
  19.3 28.1 %copy-start.3 = (bf16[448,256]{1,0:T(8,128)(2,1)S(1)}, bf16[448,256]{1,0:T(8,128)(2,1)}, u32[]{:S(2)}) copy-start(bf16[448,256]{1,0:T(8,128)(2,1)} %constant.15.clone.mats_in) | copy-start | bytes 688132
  19.3 28.0 %copy-start.6 = (f32[64]{0:T(128)S(1)}, f32[64]{0:T(128)}, u32[]{:S(2)}) copy-start(f32[64]{0:T(128)} %param.11) | copy-start | bytes 772
  21.1 29.2 %all-to-all-start = ((bf16[64,32,128]{2,1,0:T(8,128)(2,1)}), bf16[64,32,128]{2,1,0:T(8,128)(2,1)S(1)}, u32[]{:S(2)}, u32[]{:S(2)}) async-start(bf16[64,32,128]{2,1,0:T(8,128)(2,1)} %gate.1), calls=%async_computation | async-start | bytes 1048576 | tf_op jit(solution)/shard_map/all_to_all | solution.py:337
  31.1 12.3 %collective-permute-start.2 = (bf16[16,32,128]{2,1,0:T(8,128)(2,1)S(1)}, bf16[16,32,128]{2,1,0:T(8,128)(2,1)S(1)}, u32[]{:S(2)}, u32[]{:S(2)}) collective-permute-start(bf16[16,32,128]{2,1,0:T(8,128)(2,1)S(1)} %pad_maximum_fusion.own), channel_id=1, source_target_pairs={{128,0},{448,64},{256,128},{64,192},{384,256},{192,320},{0,384},{3... | collective-permute-start | bytes 393224 | tf_op jit(solution)/shard_map/ppermute | solution.py:336
  38.0 6.2 %collective-permute-start.3 = (bf16[16,32,128]{2,1,0:T(8,128)(2,1)S(1)}, bf16[16,32,128]{2,1,0:T(8,128)(2,1)S(1)}, u32[]{:S(2)}, u32[]{:S(2)}) collective-permute-start(bf16[16,32,128]{2,1,0:T(8,128)(2,1)S(1)} %pad_maximum_fusion.own), channel_id=1, source_target_pairs={{64,0},{128,64},{192,128},{256,192},{320,256},{384,320},{448,384},... | collective-permute-start | bytes 393224 | tf_op jit(solution)/shard_map/ppermute | solution.py:315
  40.0 7.4 %collective-permute-start.4 = (bf16[16,32,128]{2,1,0:T(8,128)(2,1)S(1)}, bf16[16,32,128]{2,1,0:T(8,128)(2,1)S(1)}, u32[]{:S(2)}, u32[]{:S(2)}) collective-permute-start(bf16[16,32,128]{2,1,0:T(8,128)(2,1)S(1)} %pad_maximum_fusion.own), channel_id=1, source_target_pairs={{448,0},{0,64},{64,128},{128,192},{192,256},{256,320},{320,384},{3... | collective-permute-start | bytes 393224 | tf_op jit(solution)/shard_map/ppermute | solution.py:315
  47.4 2.9 %copy-start.4 = (bf16[448,256]{1,0:T(8,128)(2,1)S(1)}, bf16[448,256]{1,0:T(8,128)(2,1)}, u32[]{:S(2)}) copy-start(bf16[448,256]{1,0:T(8,128)(2,1)} %constant.15.clone.mats_in) | copy-start | bytes 688132
  50.3 17.0 %copy-start = (bf16[1,64,3,4096]{3,1,2,0:T(8,128)(2,1)S(1)}, bf16[1,64,3,4096]{3,1,2,0:T(8,128)(2,1)}, u32[]{:S(2)}) copy-start(bf16[1,64,3,4096]{3,1,2,0:T(8,128)(2,1)} %param.7) | copy-start | bytes 4718596
  55.7 29.3 %all-to-all-start.1 = ((bf16[64,32,128]{2,1,0:T(8,128)(2,1)}), bf16[64,32,128]{2,1,0:T(8,128)(2,1)S(1)}, u32[]{:S(2)}, u32[]{:S(2)}) async-start(bf16[64,32,128]{2,1,0:T(8,128)(2,1)} %convolve.1), calls=%async_computation.1 | async-start | bytes 1048576 | tf_op jit(solution)/shard_map/all_to_all | solution.py:392

commit v3 on v2

--- a/solution.py
+++ b/solution.py
@@ -109,15 +109,9 @@
     return made
 
 
-def spec_parts(spec_in, spec, step):
-    parts = [pl.ds(i, step) for i in range(0, spec.shape[0], step)]
-    return [(spec_in.at[part], spec.at[part]) for part in parts]
-
-
-def filter_kernel(place, own, across, one_on, one_back, bias, mats_in, turns_in, spec_out, data32, mid, spec, mats, turns, sems):
-    na, nr = 4 * own.shape[0], own.shape[1]
+def conv_kernel(place, own, across, one_on, one_back, bias, z, mats_in, turns_in, out, held, filt32, filt_mid, data32, mid, mid_back, spec, mats, turns, sems):
+    na, nr, _ = z.shape
     nb = 2 * nr
-    step = na // 8
     made = copies([(mats_in, mats), (turns_in, turns)], sems)
     shards = 8
     rows = na // shards
@@ -127,43 +121,7 @@
             shard = lax.rem(place[0] + start + 4 * j, shards)
             base = pl.multiple_of(shard * (rows * (nr + PAD)), 8)
             for i in range(rows):
-                data32[pl.ds(base + i * (nr + PAD), nr), :] = source[j * rows + i].astype(F32)
-    made[0].wait()
-    first = mats[0 : 2 * na, 0 : 2 * na]
-    second = mats[2 * na : 2 * na + 2 * nb, :]
-    block_stage(data32, mid, first, na, nr)
-    made[1].wait()
-    leaving = []
-    delta = bias[...]
-    delta = jnp.concatenate([delta, delta], axis=1)
-    for p in range(0, na // 2, 2):
-        cols, turn = [], []
-        for q in (p, p + 1):
-            turn.append(turn_of(turns, q))
-            re, im = turned(mid, turn[-1], q, na, nr)
-            cols.append(jnp.concatenate([re, im], axis=0))
-        both = jnp.concatenate(cols, axis=1)
-        high = both.astype(BF16)
-        low = (both - high.astype(F32)).astype(BF16)
-        got = dot(second, twice(high)) + dot(second[:, : 2 * nb], low)
-        scale = 1.0 / (na * nb)
-        for j, q in enumerate((p, p + 1)):
-            spec[q, pl.ds(0, nb), :] = ((got[:nb, j * 128 : (j + 1) * 128] + delta) * scale).astype(BF16)
-            spec[q, pl.ds(nb, nb), :] = (got[nb:, j * 128 : (j + 1) * 128] * scale).astype(BF16)
-        if (p + 2) % step == 0:
-            part = pl.ds(p + 2 - step, step)
-            leave = pltpu.make_async_copy(spec.at[part], spec_out.at[part], sems.at[2 + p // step])
-            leave.start()
-            leaving.append(leave)
-    for leave in leaving:
-        leave.wait()
-
-
-def conv_kernel(z, spec_in, mats_in, turns_in, out, held, data32, mid, mid_back, spec, mats, turns, sems):
-    na, nr, _ = z.shape
-    nb = 2 * nr
-    step = na // 8
-    made = copies([(mats_in, mats), (turns_in, turns)] + spec_parts(spec_in, spec, step), sems)
+                filt32[pl.ds(base + i * (nr + PAD), nr), :] = source[j * rows + i].astype(F32)
     spread(z, data32)
     made[0].wait()
     at = 2 * na
@@ -171,12 +129,21 @@
     second = mats[at : at + 2 * nb, :]
     second_back = mats[at + 2 * nb : at + 4 * nb, :]
     first_back = mats[at + 4 * nb :, :]
+    block_stage(filt32, filt_mid, first, na, nr)
     block_stage(data32, mid, first, na, nr)
+    made[1].wait()
+    delta = bias[...]
+    delta = jnp.concatenate([delta, delta], axis=1)
+    scale = 1.0 / (na * nb)
     for p in range(0, na // 2, 2):
-        if p == 0:
-            made[1].wait()
-        if p % step == 0:
-            made[2 + p // step].wait()
+        cols = []
+        for q in (p, p + 1):
+            cols.append(jnp.concatenate(turned(filt_mid, turn_of(turns, q), q, na, nr), axis=0))
+        got = dot(second, twice(jnp.concatenate(cols, axis=1).astype(BF16)))
+        for j, q in enumerate((p, p + 1)):
+            spec[q, pl.ds(0, nb), :] = (got[:nb, j * 128 : (j + 1) * 128] + delta) * scale
+            spec[q, pl.ds(nb, nb), :] = got[nb:, j * 128 : (j + 1) * 128] * scale
+    for p in range(0, na // 2, 2):
         cols, turn = [], []
         for q in (p, p + 1):
             turn.append(turn_of(turns, q))
@@ -186,7 +153,7 @@
         cols = []
         for j, q in enumerate((p, p + 1)):
             re, im = got[:nb, j * 128 : (j + 1) * 128], got[nb:, j * 128 : (j + 1) * 128]
-            sre, sim = spec[q, pl.ds(0, nb), :].astype(F32), spec[q, pl.ds(nb, nb), :].astype(F32)
+            sre, sim = spec[q, pl.ds(0, nb), :], spec[q, pl.ds(nb, nb), :]
             cols.append(jnp.concatenate([re * sre - im * sim, re * sim + im * sre], axis=0))
         got = dot(second_back, twice(jnp.concatenate(cols, axis=1).astype(BF16)))
         for j, q in enumerate((p, p + 1)):
@@ -353,42 +320,28 @@
     )(alive, parts, halo, short_weight)
 
     table_scratch = [
-        pltpu.VMEM((nseq // 2, 2 * tok, 2 * chans), BF16),
+        pltpu.VMEM((nseq // 2, 2 * tok, 2 * chans), F32),
         pltpu.VMEM(mats.shape, BF16),
         pltpu.VMEM(turns.shape, F32),
     ]
-    spec = pl.pallas_call(
-        filter_kernel,
-        out_shape=jax.ShapeDtypeStruct((nseq // 2, 2 * tok, 2 * chans), BF16),
-        in_specs=[pl.BlockSpec(memory_space=pltpu.SMEM)] + vmem(5) + [hbm] * 2,
-        out_specs=hbm,
-        scratch_shapes=[
-            pltpu.VMEM((nseq * (half + PAD), 128), F32),
-            pltpu.VMEM((half * (2 * nseq + PAD), 128), F32),
-            *table_scratch,
-            pltpu.SemaphoreType.DMA((6,)),
-        ],
-        compiler_params=params(52),
-        cost_estimate=pl.CostEstimate(flops=2000000000, bytes_accessed=6000000, transcendentals=0),
-        name="filter_spectrum",
-    )(group[None], two, *others, filter_bias[None], mats, turns)
-
     y = pl.pallas_call(
         conv_kernel,
         out_shape=jax.ShapeDtypeStruct((nseq, half, 2 * chans), BF16),
-        in_specs=vmem(1) + [hbm] * 3,
+        in_specs=[pl.BlockSpec(memory_space=pltpu.SMEM)] + vmem(6) + [hbm] * 2,
         out_specs=hbm,
         scratch_shapes=[
             pltpu.VMEM((nseq, half, 2 * chans), BF16),
             pltpu.VMEM((nseq * (half + PAD), 128), F32),
             pltpu.VMEM((half * (2 * nseq + PAD), 128), F32),
+            pltpu.VMEM((nseq * (half + PAD), 128), F32),
+            pltpu.VMEM((half * (2 * nseq + PAD), 128), F32),
             pltpu.VMEM((nseq // 2 * (2 * tok + PAD), 128), F32),
             *table_scratch,
-            pltpu.SemaphoreType.DMA((6,)),
+            pltpu.SemaphoreType.DMA((4,)),
         ],
         compiler_params=params(52),
         name="convolve",
-    )(z, spec, mats, turns)
+    )(group[None], two, *others, filter_bias[None], z, mats, turns)
     y = lax.all_to_all(y, "seq", split_axis=0, concat_axis=0, tiled=True)
 
     out = pl.pallas_call(

time: 86.4 us -> 83.6 us (0.968)
  Pallas kernels: 11.7 us -> 9 us
  starting transfers between devices: 48.9 us -> 47.5 us
  waiting for transfers between devices: 21.1 us -> 22.5 us
    pallas_call x1 -> x0, Pallas kernels: 2.88 us -> none  [per_device(): pl.pallas_call(filter_kernel, out_shape=jax.ShapeDtypeStruct((nseq // 2,...]
    all_to_all x1, waiting for transfers between devices: 0.01 us -> 1.4 us  [per_device(): z = lax.all_to_all(z, 'seq', split_axis=0, concat_axis=0, tiled=True)]
    all_to_all x1, starting transfers between devices: 11.6 us -> 10.2 us  [per_device(): y = lax.all_to_all(y, 'seq', split_axis=0, concat_axis=0, tiled=True)]
  transfers between devices with their start and end apart: 7 -> 7, of which waited for: 3 -> 4; matrix products, arithmetic and copies ran while one was open for 2% -> 2% of each run, Pallas kernels for 6% -> 3%
where the time goes in v3:
time: 83.6 us; the launch traced here: 83.1 us
  starting transfers between devices  47.5 us (57%)
  waiting for transfers between devices  22.5 us (27%)
  Pallas kernels  9 us (11%)
  local copies, waits for them, and re-layouts  3.26 us (4%)
  between operations  0.84 us (1%)
    all_to_all x1, waiting for transfers between devices, per_device(): y = lax.all_to_all(y, 'seq', split_axis=0, concat_axis=0, tiled=True)  17.1 us
    ppermute x3, starting transfers between devices, from_shift(): lax.ppermute(x, 'grp', [((i + shift) % ngrp, i) for i in range(ngrp)])  15.9 us
    all_to_all x1, starting transfers between devices, per_device(): y = lax.all_to_all(y, 'seq', split_axis=0, concat_axis=0, tiled=True)  10.2 us
    all_to_all x1, starting transfers between devices, per_device(): z = lax.all_to_all(z, 'seq', split_axis=0, concat_axis=0, tiled=True)  9.95 us
    ppermute x1, starting transfers between devices, per_device(): lax.ppermute(two, 'grp', across)  6.98 us
    pallas_call x1, Pallas kernels, per_device(): pl.pallas_call(conv_kernel, out_shape=jax.ShapeDtypeStruct((nseq, half, 2...  5.48 us
    ppermute x1, starting transfers between devices, per_device(): halo = lax.ppermute(last, 'seq', [(i, i + 1) for i in range(nseq - 1)])  4.51 us
    ppermute x3, waiting for transfers between devices, from_shift(): lax.ppermute(x, 'grp', [((i + shift) % ngrp, i) for i in range(ngrp)])  4.02 us
  transfers between devices with their start and end apart: 7, of which 4 were waited for; matrix products, arithmetic and copies ran while one was open for 2% of the time, Pallas kernels for 3%

profile of v3, /device:TPU:1, one launch (start us, length us, event | category | flops | bytes accessed | tf_op | source)
XLA Modules:
  0.0 83.1 jit_solution(8213231031323832130)
XLA Ops:
  0.0 0.0 copy-start.1
  0.0 1.0 %slice.13 = bf16[3,2,4096]{2,1,0:T(2,128)(2,1)S(1)} slice(bf16[3,64,4096]{2,1,0:T(8,128)(2,1)} %bitcast.7), slice={[0:3], [62:64], [0:4096]} | slice | bytes 98304 | tf_op jit(solution)/shard_map/slice | solution.py:267
  1.0 4.5 %collective-permute-start = (bf16[3,2,4096]{2,1,0:T(2,128)(2,1)S(1)}, bf16[3,2,4096]{2,1,0:T(2,128)(2,1)S(1)}, u32[]{:S(2)}, u32[]{:S(2)}) collective-permute-start(bf16[3,2,4096]{2,1,0:T(2,128)(2,1)S(1)} %slice.13), channel_id=1, source_target_pairs={{0,1},{1,2},{2,3},{3,4},{4,5},{5,6},{6,7},{7,8},{8,9},{9,10},{10,1... | collective-permute-start | bytes 147464 | tf_op jit(solution)/shard_map/ppermute | solution.py:268
  5.5 0.0 copy-start.3
  5.6 0.9 %copy-done.3 = f32[64,512]{1,0:T(8,128)S(1)} copy-done((f32[64,512]{1,0:T(8,128)S(1)}, f32[64,512]{1,0:T(8,128)}, u32[]{:S(2)}) %copy-start.3) | copy-done | bytes 131096
  6.5 0.2 turn_filter.1
  6.7 10.6 %collective-permute-start.1 = (bf16[8,32,128]{2,1,0:T(8,128)(2,1)S(1)}, bf16[8,32,128]{2,1,0:T(8,128)(2,1)S(1)}, u32[]{:S(2)}, u32[]{:S(2)}) collective-permute-start(bf16[8,32,128]{2,1,0:T(8,128)(2,1)S(1)} %turn_filter.1), channel_id=1, source_target_pairs={{256,0},{320,64},{384,128},{448,192},{0,256},{64,320},{128,384},{1... | collective-permute-start | bytes 196616 | tf_op jit(solution)/shard_map/ppermute | solution.py:282
  17.3 1.3 %slice.12.rows = bf16[2,64,4096]{2,1,0:T(8,128)(2,1)S(1)} slice(bf16[3,64,4096]{2,1,0:T(8,128)(2,1)} %bitcast.8), slice={[1:3], [0:64], [0:4096]} | slice | bytes 2097152 | tf_op jit(solution)/shard_map/slice | solution.py:285
  19.3 0.0 copy-done.1
  19.3 0.0 copy-start.2
  19.3 0.0 copy-start.4
  19.3 0.0 collective-permute-done.halo
  19.3 1.7 %gate.1 = bf16[64,32,128]{2,1,0:T(8,128)(2,1)} custom-call(s32[1]{0:T(128)S(6)} %sub.7.alive, bf16[2,64,4096]{2,1,0:T(8,128)(2,1)S(1)} %slice.12.rows, bf16[3,2,4096]{2,1,0:T(2,128)(2,1)S(1)} %collective-permute-done.halo, f32[2,3,4096]{2,1,0:T(4,128)S(1)} %slice.11.weights), custom_call_target="tpu_custom_call" | custom-call | flops 1000000000 | bytes 2000000 | tf_op jit(solution)/shard_map/gate/pallas_call | solution.py:288
  21.1 0.0 collective-permute-done.1
  21.1 9.9 %all-to-all-start = ((bf16[64,32,128]{2,1,0:T(8,128)(2,1)}), bf16[64,32,128]{2,1,0:T(8,128)(2,1)S(1)}, u32[]{:S(2)}, u32[]{:S(2)}) async-start(bf16[64,32,128]{2,1,0:T(8,128)(2,1)} %gate.1), calls=%async_computation | async-start | bytes 1048576 | tf_op jit(solution)/shard_map/all_to_all | solution.py:304
  31.1 7.0 %collective-permute-start.2 = (bf16[16,32,128]{2,1,0:T(8,128)(2,1)S(1)}, bf16[16,32,128]{2,1,0:T(8,128)(2,1)S(1)}, u32[]{:S(2)}, u32[]{:S(2)}) collective-permute-start(bf16[16,32,128]{2,1,0:T(8,128)(2,1)S(1)} %pad_maximum_fusion.own), channel_id=1, source_target_pairs={{128,0},{448,64},{256,128},{64,192},{384,256},{192,320},{0,384},{3... | collective-permute-start | bytes 393224 | tf_op jit(solution)/shard_map/ppermute | solution.py:303
  38.0 1.9 %collective-permute-start.3 = (bf16[16,32,128]{2,1,0:T(8,128)(2,1)S(1)}, bf16[16,32,128]{2,1,0:T(8,128)(2,1)S(1)}, u32[]{:S(2)}, u32[]{:S(2)}) collective-permute-start(bf16[16,32,128]{2,1,0:T(8,128)(2,1)S(1)} %pad_maximum_fusion.own), channel_id=1, source_target_pairs={{64,0},{128,64},{192,128},{256,192},{320,256},{384,320},{448,384},... | collective-permute-start | bytes 393224 | tf_op jit(solution)/shard_map/ppermute | solution.py:282
  40.0 3.4 %collective-permute-start.4 = (bf16[16,32,128]{2,1,0:T(8,128)(2,1)S(1)}, bf16[16,32,128]{2,1,0:T(8,128)(2,1)S(1)}, u32[]{:S(2)}, u32[]{:S(2)}) collective-permute-start(bf16[16,32,128]{2,1,0:T(8,128)(2,1)S(1)} %pad_maximum_fusion.own), channel_id=1, source_target_pairs={{448,0},{0,64},{64,128},{128,192},{192,256},{256,320},{320,384},{3... | collective-permute-start | bytes 393224 | tf_op jit(solution)/shard_map/ppermute | solution.py:282
  43.4 0.0 collective-permute-done.2.across
  43.4 0.9 %collective-permute-done.3.one_on = bf16[16,32,128]{2,1,0:T(8,128)(2,1)S(1)} collective-permute-done((bf16[16,32,128]{2,1,0:T(8,128)(2,1)S(1)}, bf16[16,32,128]{2,1,0:T(8,128)(2,1)S(1)}, u32[]{:S(2)}, u32[]{:S(2)}) %collective-permute-start.3) | collective-permute-done | bytes 131104 | tf_op jit(solution)/shard_map/ppermute | solution.py:282
  44.2 3.1 %collective-permute-done.4.one_back = bf16[16,32,128]{2,1,0:T(8,128)(2,1)S(1)} collective-permute-done((bf16[16,32,128]{2,1,0:T(8,128)(2,1)S(1)}, bf16[16,32,128]{2,1,0:T(8,128)(2,1)S(1)}, u32[]{:S(2)}, u32[]{:S(2)}) %collective-permute-start.4) | collective-permute-done | bytes 131104 | tf_op jit(solution)/shard_map/ppermute | solution.py:282
  47.4 1.4 %all-to-all-done.z = bf16[64,32,128]{2,1,0:T(8,128)(2,1)S(1)} async-done(((bf16[64,32,128]{2,1,0:T(8,128)(2,1)}), bf16[64,32,128]{2,1,0:T(8,128)(2,1)S(1)}, u32[]{:S(2)}, u32[]{:S(2)}) %all-to-all-start) | async-done | bytes 524320 | tf_op jit(solution)/shard_map/all_to_all | solution.py:304
  48.8 0.0 copy-done.2
  48.8 0.0 copy-done.4
  48.8 0.0 copy-start
  48.8 5.5 %convolve.1 = bf16[64,32,128]{2,1,0:T(8,128)(2,1)} custom-call(s32[1]{0:T(128)} %bitcast.place, bf16[16,32,128]{2,1,0:T(8,128)(2,1)S(1)} %pad_maximum_fusion.own, bf16[16,32,128]{2,1,0:T(8,128)(2,1)S(1)} %collective-permute-done.2.across, bf16[16,32,128]{2,1,0:T(8,128)(2,1)S(1)} %collective-permute-done.3.one_on, ...), custom_call_target="tpu_custom_call" | custom-call | tf_op jit(solution)/shard_map/convolve/pallas_call | solution.py:327
  54.3 10.2 %all-to-all-start.1 = ((bf16[64,32,128]{2,1,0:T(8,128)(2,1)}), bf16[64,32,128]{2,1,0:T(8,128)(2,1)S(1)}, u32[]{:S(2)}, u32[]{:S(2)}) async-start(bf16[64,32,128]{2,1,0:T(8,128)(2,1)} %convolve.1), calls=%async_computation.1 | async-start | bytes 1048576 | tf_op jit(solution)/shard_map/all_to_all | solution.py:345
  64.5 0.0 copy-done
  64.5 0.6 query.1
  65.1 17.1 %all-to-all-done.1.y = bf16[64,32,128]{2,1,0:T(8,128)(2,1)S(1)} async-done(((bf16[64,32,128]{2,1,0:T(8,128)(2,1)}), bf16[64,32,128]{2,1,0:T(8,128)(2,1)S(1)}, u32[]{:S(2)}, u32[]{:S(2)}) %all-to-all-start.1) | async-done | bytes 524320 | tf_op jit(solution)/shard_map/all_to_all | solution.py:345
  82.2 1.0 %mix.1 = bf16[64,4096]{1,0:T(8,128)(2,1)} custom-call(bf16[64,32,128]{2,1,0:T(8,128)(2,1)S(1)} %all-to-all-done.1.y, f32[64,4096]{1,0:T(8,128)S(1)} %query.1), custom_call_target="tpu_custom_call" | custom-call | tf_op jit(solution)/shard_map/mix/pallas_call | solution.py:347
  (2 shorter events, 0.0 us)
Async XLA Ops:
  0.0 19.3 %copy-start.1 = (f32[3,3,4096]{2,1,0:T(4,128)S(1)}, f32[3,3,4096]{2,1,0:T(4,128)}, u32[]{:S(2)}) copy-start(f32[3,3,4096]{2,1,0:T(4,128)} %weights.1) | copy-start | bytes 442372
  1.0 18.3 %collective-permute-start = (bf16[3,2,4096]{2,1,0:T(2,128)(2,1)S(1)}, bf16[3,2,4096]{2,1,0:T(2,128)(2,1)S(1)}, u32[]{:S(2)}, u32[]{:S(2)}) collective-permute-start(bf16[3,2,4096]{2,1,0:T(2,128)(2,1)S(1)} %slice.13), channel_id=1, source_target_pairs={{0,1},{1,2},{2,3},{3,4},{4,5},{5,6},{6,7},{7,8},{8,9},{9,10},{10,1... | collective-permute-start | bytes 147464 | tf_op jit(solution)/shard_map/ppermute | solution.py:268
  5.5 0.9 %copy-start.3 = (f32[64,512]{1,0:T(8,128)S(1)}, f32[64,512]{1,0:T(8,128)}, u32[]{:S(2)}) copy-start(f32[64,512]{1,0:T(8,128)} %filt) | copy-start | bytes 393220
  6.7 14.4 %collective-permute-start.1 = (bf16[8,32,128]{2,1,0:T(8,128)(2,1)S(1)}, bf16[8,32,128]{2,1,0:T(8,128)(2,1)S(1)}, u32[]{:S(2)}, u32[]{:S(2)}) collective-permute-start(bf16[8,32,128]{2,1,0:T(8,128)(2,1)S(1)} %turn_filter.1), channel_id=1, source_target_pairs={{256,0},{320,64},{384,128},{448,192},{0,256},{64,320},{128,384},{1... | collective-permute-start | bytes 196616 | tf_op jit(solution)/shard_map/ppermute | solution.py:282
  19.3 29.5 %copy-start.2 = (bf16[448,256]{1,0:T(8,128)(2,1)S(1)}, bf16[448,256]{1,0:T(8,128)(2,1)}, u32[]{:S(2)}) copy-start(bf16[448,256]{1,0:T(8,128)(2,1)} %constant.15.clone.mats_in) | copy-start | bytes 688132
  19.3 29.5 %copy-start.4 = (f32[64]{0:T(128)S(1)}, f32[64]{0:T(128)}, u32[]{:S(2)}) copy-start(f32[64]{0:T(128)} %param.11) | copy-start | bytes 772
  21.1 27.7 %all-to-all-start = ((bf16[64,32,128]{2,1,0:T(8,128)(2,1)}), bf16[64,32,128]{2,1,0:T(8,128)(2,1)S(1)}, u32[]{:S(2)}, u32[]{:S(2)}) async-start(bf16[64,32,128]{2,1,0:T(8,128)(2,1)} %gate.1), calls=%async_computation | async-start | bytes 1048576 | tf_op jit(solution)/shard_map/all_to_all | solution.py:304
  31.1 12.3 %collective-permute-start.2 = (bf16[16,32,128]{2,1,0:T(8,128)(2,1)S(1)}, bf16[16,32,128]{2,1,0:T(8,128)(2,1)S(1)}, u32[]{:S(2)}, u32[]{:S(2)}) collective-permute-start(bf16[16,32,128]{2,1,0:T(8,128)(2,1)S(1)} %pad_maximum_fusion.own), channel_id=1, source_target_pairs={{128,0},{448,64},{256,128},{64,192},{384,256},{192,320},{0,384},{3... | collective-permute-start | bytes 393224 | tf_op jit(solution)/shard_map/ppermute | solution.py:303
  38.0 6.2 %collective-permute-start.3 = (bf16[16,32,128]{2,1,0:T(8,128)(2,1)S(1)}, bf16[16,32,128]{2,1,0:T(8,128)(2,1)S(1)}, u32[]{:S(2)}, u32[]{:S(2)}) collective-permute-start(bf16[16,32,128]{2,1,0:T(8,128)(2,1)S(1)} %pad_maximum_fusion.own), channel_id=1, source_target_pairs={{64,0},{128,64},{192,128},{256,192},{320,256},{384,320},{448,384},... | collective-permute-start | bytes 393224 | tf_op jit(solution)/shard_map/ppermute | solution.py:282
  40.0 7.4 %collective-permute-start.4 = (bf16[16,32,128]{2,1,0:T(8,128)(2,1)S(1)}, bf16[16,32,128]{2,1,0:T(8,128)(2,1)S(1)}, u32[]{:S(2)}, u32[]{:S(2)}) collective-permute-start(bf16[16,32,128]{2,1,0:T(8,128)(2,1)S(1)} %pad_maximum_fusion.own), channel_id=1, source_target_pairs={{448,0},{0,64},{64,128},{128,192},{192,256},{256,320},{320,384},{3... | collective-permute-start | bytes 393224 | tf_op jit(solution)/shard_map/ppermute | solution.py:282
  48.8 15.7 %copy-start = (bf16[1,64,3,4096]{3,1,2,0:T(8,128)(2,1)S(1)}, bf16[1,64,3,4096]{3,1,2,0:T(8,128)(2,1)}, u32[]{:S(2)}) copy-start(bf16[1,64,3,4096]{3,1,2,0:T(8,128)(2,1)} %param.7) | copy-start | bytes 4718596
  54.3 27.9 %all-to-all-start.1 = ((bf16[64,32,128]{2,1,0:T(8,128)(2,1)}), bf16[64,32,128]{2,1,0:T(8,128)(2,1)S(1)}, u32[]{:S(2)}, u32[]{:S(2)}) async-start(bf16[64,32,128]{2,1,0:T(8,128)(2,1)} %convolve.1), calls=%async_computation.1 | async-start | bytes 1048576 | tf_op jit(solution)/shard_map/all_to_all | solution.py:345

commit v4 on v3

--- a/solution.py
+++ b/solution.py
@@ -203,14 +203,19 @@
     return weights[0:1] * x + weights[1:2] * back1 + weights[2:3] * back2
 
 
-def gate_kernel(alive, rows, halo, weights, out, held, sems):
+def gate_kernel(alive, rows_in, halo, weights_in, out, rows, weights, held, in_sems, sems):
     count = rows.shape[2] // 128
     step = count // 4
+    spans = [pl.ds(i * step * 128, step * 128) for i in range(4)]
+    coming = copies([(weights_in, weights)] + [(rows_in.at[pl.ds(1, 2), :, span], rows.at[:, :, span]) for span in spans], in_sems)
+    coming[0].wait()
     made = []
     for i in range(count):
+        if i % step == 0:
+            coming[1 + i // step].wait()
         at = pl.ds(i * 128, 128)
-        key = short_sum(rows[0, :, at], halo[1, :, at], weights[0, :, at], alive[0])
-        val = short_sum(rows[1, :, at], halo[2, :, at], weights[1, :, at], alive[0])
+        key = short_sum(rows[0, :, at], halo[1, :, at], weights[1, :, at], alive[0])
+        val = short_sum(rows[1, :, at], halo[2, :, at], weights[2, :, at], alive[0])
         z = key * val
         half = z.shape[0] // 2
         one, two = lane_mix(z[:half], z[half:])
@@ -264,8 +269,7 @@
     span = long_filter.shape[1]
     parts = jnp.transpose(rows[0], (1, 0, 2))
     alive = lengths - me * tok
-    last, long_filter = lax.optimization_barrier((parts[:, tok - 2 :, :], long_filter))
-    halo = lax.ppermute(last, "seq", [(i, i + 1) for i in range(nseq - 1)])
+    halo = lax.ppermute(parts[:, tok - 2 :, :], "seq", [(i, i + 1) for i in range(nseq - 1)])
     mats, turns = [jnp.asarray(t) for t in transform_tables(nseq, tok)]
 
     own = pl.pallas_call(
@@ -282,22 +286,24 @@
         return lax.ppermute(x, "grp", [((i + shift) % ngrp, i) for i in range(ngrp)])
 
     two = jnp.concatenate([own, from_shift(own, 4)], axis=0)
-    pair = parts[1:]
     hbm = pl.BlockSpec(memory_space=pltpu.HBM)
     block = 1024
     z = pl.pallas_call(
         gate_kernel,
         out_shape=jax.ShapeDtypeStruct((nseq, half, 2 * chans), BF16),
-        in_specs=[pl.BlockSpec(memory_space=pltpu.SMEM)] + vmem(3),
+        in_specs=[pl.BlockSpec(memory_space=pltpu.SMEM), hbm] + vmem(1) + [hbm],
         out_specs=hbm,
         scratch_shapes=[
+            pltpu.VMEM((2, tok, width), BF16),
+            pltpu.VMEM(short_weight.shape, F32),
             pltpu.VMEM((nseq, half, 2 * chans), BF16),
+            pltpu.SemaphoreType.DMA((5,)),
             pltpu.SemaphoreType.DMA((4,)),
         ],
-        compiler_params=params(48),
+        compiler_params=params(53),
         cost_estimate=pl.CostEstimate(flops=1000000000, bytes_accessed=2000000, transcendentals=0),
         name="gate",
-    )(alive, pair, halo, short_weight[1:])
+    )(alive, parts, halo, short_weight)
     z, two = lax.optimization_barrier((z, two))
     across = [((i + (2 if i % 2 == 0 else 6)) % ngrp, i) for i in range(ngrp)]
     others = [lax.ppermute(two, "grp", across), from_shift(two, 1), from_shift(two, 7)]

time: 83.6 us -> 82.1 us (0.982)
  starting transfers between devices: 47.5 us -> 43.8 us
  Pallas kernels: 9 us -> 10.5 us
  waiting for transfers between devices: 22.5 us -> 23.6 us
    ppermute x3, waiting for transfers between devices: 4.02 us -> 0.01 us  [from_shift(): lax.ppermute(x, 'grp', [((i + shift) % ngrp, i) for i in range(ngrp)])]
    all_to_all x1, waiting for transfers between devices: 1.4 us -> 4.2 us  [per_device(): z = lax.all_to_all(z, 'seq', split_axis=0, concat_axis=0, tiled=True)]
    all_to_all x1, starting transfers between devices: 10.2 us -> 7.55 us  [per_device(): y = lax.all_to_all(y, 'seq', split_axis=0, concat_axis=0, tiled=True)]
    ppermute x1, starting transfers between devices: 6.98 us -> 4.56 us  [per_device(): lax.ppermute(two, 'grp', across)]
    ppermute x1, waiting for transfers between devices: 0.01 us -> 2.31 us  [per_device(): lax.ppermute(two, 'grp', across)]
    pallas_call x1, Pallas kernels: 1.71 us -> 3.21 us  [per_device(): pl.pallas_call(gate_kernel, out_shape=jax.ShapeDtypeStruct((nseq, half, 2...]
    slice x2 -> x0, local copies, waits for them, and re-layouts: 1.32 us -> none  [the longest x1 1.3 us: per_device(): pair = parts[1:]]
    ppermute x3, starting transfers between devices: 15.9 us -> 17.2 us  [from_shift(): lax.ppermute(x, 'grp', [((i + shift) % ngrp, i) for i in range(ngrp)])]
  transfers between devices with their start and end apart: 7 -> 7, of which waited for: 4 -> 3; matrix products, arithmetic and copies ran while one was open for 2% -> 0% of each run, Pallas kernels for 3% -> 5%
where the time goes in v4:
time: 82.1 us; the launch traced here: 81.6 us
  starting transfers between devices  43.8 us (53%)
  waiting for transfers between devices  23.6 us (29%)
  Pallas kernels  10.5 us (13%)
  local copies, waits for them, and re-layouts  2.86 us (3%)
  between operations  0.84 us (1%)
    ppermute x3, starting transfers between devices, from_shift(): lax.ppermute(x, 'grp', [((i + shift) % ngrp, i) for i in range(ngrp)])  17.2 us
    all_to_all x1, waiting for transfers between devices, per_device(): y = lax.all_to_all(y, 'seq', split_axis=0, concat_axis=0, tiled=True)  17 us
    all_to_all x1, starting transfers between devices, per_device(): z = lax.all_to_all(z, 'seq', split_axis=0, concat_axis=0, tiled=True)  9.95 us
    all_to_all x1, starting transfers between devices, per_device(): y = lax.all_to_all(y, 'seq', split_axis=0, concat_axis=0, tiled=True)  7.55 us
    pallas_call x1, Pallas kernels, per_device(): pl.pallas_call(conv_kernel, out_shape=jax.ShapeDtypeStruct((nseq, half, 2...  5.53 us
    ppermute x1, starting transfers between devices, per_device(): lax.ppermute(two, 'grp', across)  4.56 us
    ppermute x1, starting transfers between devices, per_device(): lax.ppermute(parts[:, tok - 2:, :], 'seq', [(i, i + 1) for i in range(nse...  4.51 us
    all_to_all x1, waiting for transfers between devices, per_device(): z = lax.all_to_all(z, 'seq', split_axis=0, concat_axis=0, tiled=True)  4.2 us
  transfers between devices with their start and end apart: 7, of which 3 were waited for; matrix products, arithmetic and copies ran while one was open for 0% of the time, Pallas kernels for 5%

profile of v4, /device:TPU:1, one launch (start us, length us, event | category | flops | bytes accessed | tf_op | source)
XLA Modules:
  0.0 81.6 jit_solution(16702828769563999769)
XLA Ops:
  0.0 1.0 %slice.4 = bf16[3,2,4096]{2,1,0:T(2,128)(2,1)S(1)} slice(bf16[3,64,4096]{2,1,0:T(8,128)(2,1)} %bitcast.7), slice={[0:3], [62:64], [0:4096]} | slice | bytes 98304 | tf_op jit(solution)/shard_map/slice | solution.py:272
  1.0 4.5 %collective-permute-start = (bf16[3,2,4096]{2,1,0:T(2,128)(2,1)S(1)}, bf16[3,2,4096]{2,1,0:T(2,128)(2,1)S(1)}, u32[]{:S(2)}, u32[]{:S(2)}) collective-permute-start(bf16[3,2,4096]{2,1,0:T(2,128)(2,1)S(1)} %slice.4), channel_id=1, source_target_pairs={{0,1},{1,2},{2,3},{3,4},{4,5},{5,6},{6,7},{7,8},{8,9},{9,10},{10,1... | collective-permute-start | bytes 147464 | tf_op jit(solution)/shard_map/ppermute | solution.py:272
  5.5 0.0 copy-start.4
  5.5 0.9 %copy-done.4 = f32[64,512]{1,0:T(8,128)S(1)} copy-done((f32[64,512]{1,0:T(8,128)S(1)}, f32[64,512]{1,0:T(8,128)}, u32[]{:S(2)}) %copy-start.4) | copy-done | bytes 131096
  6.4 0.2 turn_filter.1
  6.6 10.6 %collective-permute-start.1 = (bf16[8,32,128]{2,1,0:T(8,128)(2,1)S(1)}, bf16[8,32,128]{2,1,0:T(8,128)(2,1)S(1)}, u32[]{:S(2)}, u32[]{:S(2)}) collective-permute-start(bf16[8,32,128]{2,1,0:T(8,128)(2,1)S(1)} %turn_filter.1), channel_id=1, source_target_pairs={{256,0},{320,64},{384,128},{448,192},{0,256},{64,320},{128,384},{1... | collective-permute-start | bytes 196616 | tf_op jit(solution)/shard_map/ppermute | solution.py:286
  17.9 0.0 copy-start.1
  17.9 0.0 collective-permute-done.halo
  17.9 0.0 copy-start.2
  18.0 1.0 %copy-done.2 = f32[3,3,4096]{2,1,0:T(4,128)S(1)} copy-done((f32[3,3,4096]{2,1,0:T(4,128)S(1)}, f32[3,3,4096]{2,1,0:T(4,128)}, u32[]{:S(2)}) %copy-start.2) | copy-done | bytes 147480
  18.9 0.0 copy-start.5
  18.9 3.2 %gate.1 = bf16[64,32,128]{2,1,0:T(8,128)(2,1)} custom-call(s32[1]{0:T(128)S(6)} %sub.7.alive, bf16[3,64,4096]{2,1,0:T(8,128)(2,1)} %bitcast.8, bf16[3,2,4096]{2,1,0:T(2,128)(2,1)S(1)} %collective-permute-done.halo, f32[3,3,4096]{2,1,0:T(4,128)S(1)} %copy-done.2), custom_call_target="tpu_custom_call" | custom-call | flops 1000000000 | bytes 2000000 | tf_op jit(solution)/shard_map/gate/pallas_call | solution.py:291
  22.1 0.0 collective-permute-done.1
  22.2 9.9 %all-to-all-start = ((bf16[64,32,128]{2,1,0:T(8,128)(2,1)}), bf16[64,32,128]{2,1,0:T(8,128)(2,1)S(1)}, u32[]{:S(2)}, u32[]{:S(2)}) async-start(bf16[64,32,128]{2,1,0:T(8,128)(2,1)} %gate.1), calls=%async_computation | async-start | bytes 1048576 | tf_op jit(solution)/shard_map/all_to_all | solution.py:310
  32.1 3.1 %collective-permute-start.4 = (bf16[16,32,128]{2,1,0:T(8,128)(2,1)S(1)}, bf16[16,32,128]{2,1,0:T(8,128)(2,1)S(1)}, u32[]{:S(2)}, u32[]{:S(2)}) collective-permute-start(bf16[16,32,128]{2,1,0:T(8,128)(2,1)S(1)} %pad_maximum_fusion.own), channel_id=1, source_target_pairs={{448,0},{0,64},{64,128},{128,192},{192,256},{256,320},{320,384},{3... | collective-permute-start | bytes 393224 | tf_op jit(solution)/shard_map/ppermute | solution.py:286
  35.2 3.5 %collective-permute-start.3 = (bf16[16,32,128]{2,1,0:T(8,128)(2,1)S(1)}, bf16[16,32,128]{2,1,0:T(8,128)(2,1)S(1)}, u32[]{:S(2)}, u32[]{:S(2)}) collective-permute-start(bf16[16,32,128]{2,1,0:T(8,128)(2,1)S(1)} %pad_maximum_fusion.own), channel_id=1, source_target_pairs={{64,0},{128,64},{192,128},{256,192},{320,256},{384,320},{448,384},... | collective-permute-start | bytes 393224 | tf_op jit(solution)/shard_map/ppermute | solution.py:286
  38.7 4.6 %collective-permute-start.2 = (bf16[16,32,128]{2,1,0:T(8,128)(2,1)S(1)}, bf16[16,32,128]{2,1,0:T(8,128)(2,1)S(1)}, u32[]{:S(2)}, u32[]{:S(2)}) collective-permute-start(bf16[16,32,128]{2,1,0:T(8,128)(2,1)S(1)} %pad_maximum_fusion.own), channel_id=1, source_target_pairs={{128,0},{448,64},{256,128},{64,192},{384,256},{192,320},{0,384},{3... | collective-permute-start | bytes 393224 | tf_op jit(solution)/shard_map/ppermute | solution.py:309
  43.3 0.0 collective-permute-done.4.one_back
  43.3 0.0 collective-permute-done.3.one_on
  43.3 2.3 %collective-permute-done.2.across = bf16[16,32,128]{2,1,0:T(8,128)(2,1)S(1)} collective-permute-done((bf16[16,32,128]{2,1,0:T(8,128)(2,1)S(1)}, bf16[16,32,128]{2,1,0:T(8,128)(2,1)S(1)}, u32[]{:S(2)}, u32[]{:S(2)}) %collective-permute-start.2) | collective-permute-done | bytes 131104 | tf_op jit(solution)/shard_map/ppermute | solution.py:309
  45.6 4.2 %all-to-all-done.z = bf16[64,32,128]{2,1,0:T(8,128)(2,1)S(1)} async-done(((bf16[64,32,128]{2,1,0:T(8,128)(2,1)}), bf16[64,32,128]{2,1,0:T(8,128)(2,1)S(1)}, u32[]{:S(2)}, u32[]{:S(2)}) %all-to-all-start) | async-done | bytes 524320 | tf_op jit(solution)/shard_map/all_to_all | solution.py:310
  49.8 0.0 copy-done.1
  49.8 0.0 copy-done.5
  49.8 0.0 copy-start
  49.8 0.0 copy-start.3
  49.9 5.5 %convolve.1 = bf16[64,32,128]{2,1,0:T(8,128)(2,1)} custom-call(s32[1]{0:T(128)} %bitcast.place, bf16[16,32,128]{2,1,0:T(8,128)(2,1)S(1)} %pad_maximum_fusion.own, bf16[16,32,128]{2,1,0:T(8,128)(2,1)S(1)} %collective-permute-done.2.across, bf16[16,32,128]{2,1,0:T(8,128)(2,1)S(1)} %collective-permute-done.3.one_on, ...), custom_call_target="tpu_custom_call" | custom-call | tf_op jit(solution)/shard_map/convolve/pallas_call | solution.py:333
  55.4 7.6 %all-to-all-start.1 = ((bf16[64,32,128]{2,1,0:T(8,128)(2,1)}), bf16[64,32,128]{2,1,0:T(8,128)(2,1)S(1)}, u32[]{:S(2)}, u32[]{:S(2)}) async-start(bf16[64,32,128]{2,1,0:T(8,128)(2,1)} %convolve.1), calls=%async_computation.1 | async-start | bytes 1048576 | tf_op jit(solution)/shard_map/all_to_all | solution.py:351
  63.0 0.0 copy-done
  63.0 0.0 copy-done.3
  63.0 0.6 query.1
  63.6 17.0 %all-to-all-done.1.y = bf16[64,32,128]{2,1,0:T(8,128)(2,1)S(1)} async-done(((bf16[64,32,128]{2,1,0:T(8,128)(2,1)}), bf16[64,32,128]{2,1,0:T(8,128)(2,1)S(1)}, u32[]{:S(2)}, u32[]{:S(2)}) %all-to-all-start.1) | async-done | bytes 524320 | tf_op jit(solution)/shard_map/all_to_all | solution.py:351
  80.7 1.0 %mix.1 = bf16[64,4096]{1,0:T(8,128)(2,1)} custom-call(bf16[64,32,128]{2,1,0:T(8,128)(2,1)S(1)} %all-to-all-done.1.y, f32[64,4096]{1,0:T(8,128)S(1)} %query.1), custom_call_target="tpu_custom_call" | custom-call | tf_op jit(solution)/shard_map/mix/pallas_call | solution.py:353
  (1 shorter events, 0.0 us)
Async XLA Ops:
  1.0 17.0 %collective-permute-start = (bf16[3,2,4096]{2,1,0:T(2,128)(2,1)S(1)}, bf16[3,2,4096]{2,1,0:T(2,128)(2,1)S(1)}, u32[]{:S(2)}, u32[]{:S(2)}) collective-permute-start(bf16[3,2,4096]{2,1,0:T(2,128)(2,1)S(1)} %slice.4), channel_id=1, source_target_pairs={{0,1},{1,2},{2,3},{3,4},{4,5},{5,6},{6,7},{7,8},{8,9},{9,10},{10,1... | collective-permute-start | bytes 147464 | tf_op jit(solution)/shard_map/ppermute | solution.py:272
  5.5 0.9 %copy-start.4 = (f32[64,512]{1,0:T(8,128)S(1)}, f32[64,512]{1,0:T(8,128)}, u32[]{:S(2)}) copy-start(f32[64,512]{1,0:T(8,128)} %filt.1) | copy-start | bytes 393220
  6.6 15.5 %collective-permute-start.1 = (bf16[8,32,128]{2,1,0:T(8,128)(2,1)S(1)}, bf16[8,32,128]{2,1,0:T(8,128)(2,1)S(1)}, u32[]{:S(2)}, u32[]{:S(2)}) collective-permute-start(bf16[8,32,128]{2,1,0:T(8,128)(2,1)S(1)} %turn_filter.1), channel_id=1, source_target_pairs={{256,0},{320,64},{384,128},{448,192},{0,256},{64,320},{128,384},{1... | collective-permute-start | bytes 196616 | tf_op jit(solution)/shard_map/ppermute | solution.py:286
  17.9 31.9 %copy-start.1 = (bf16[448,256]{1,0:T(8,128)(2,1)S(1)}, bf16[448,256]{1,0:T(8,128)(2,1)}, u32[]{:S(2)}) copy-start(bf16[448,256]{1,0:T(8,128)(2,1)} %constant.15.clone.mats_in) | copy-start | bytes 688132
  17.9 1.0 %copy-start.2 = (f32[3,3,4096]{2,1,0:T(4,128)S(1)}, f32[3,3,4096]{2,1,0:T(4,128)}, u32[]{:S(2)}) copy-start(f32[3,3,4096]{2,1,0:T(4,128)} %weights.1) | copy-start | bytes 442372
  18.9 30.9 %copy-start.5 = (f32[64]{0:T(128)S(1)}, f32[64]{0:T(128)}, u32[]{:S(2)}) copy-start(f32[64]{0:T(128)} %param.11) | copy-start | bytes 772
  22.2 27.7 %all-to-all-start = ((bf16[64,32,128]{2,1,0:T(8,128)(2,1)}), bf16[64,32,128]{2,1,0:T(8,128)(2,1)S(1)}, u32[]{:S(2)}, u32[]{:S(2)}) async-start(bf16[64,32,128]{2,1,0:T(8,128)(2,1)} %gate.1), calls=%async_computation | async-start | bytes 1048576 | tf_op jit(solution)/shard_map/all_to_all | solution.py:310
  32.1 11.2 %collective-permute-start.4 = (bf16[16,32,128]{2,1,0:T(8,128)(2,1)S(1)}, bf16[16,32,128]{2,1,0:T(8,128)(2,1)S(1)}, u32[]{:S(2)}, u32[]{:S(2)}) collective-permute-start(bf16[16,32,128]{2,1,0:T(8,128)(2,1)S(1)} %pad_maximum_fusion.own), channel_id=1, source_target_pairs={{448,0},{0,64},{64,128},{128,192},{192,256},{256,320},{320,384},{3... | collective-permute-start | bytes 393224 | tf_op jit(solution)/shard_map/ppermute | solution.py:286
  35.2 8.1 %collective-permute-start.3 = (bf16[16,32,128]{2,1,0:T(8,128)(2,1)S(1)}, bf16[16,32,128]{2,1,0:T(8,128)(2,1)S(1)}, u32[]{:S(2)}, u32[]{:S(2)}) collective-permute-start(bf16[16,32,128]{2,1,0:T(8,128)(2,1)S(1)} %pad_maximum_fusion.own), channel_id=1, source_target_pairs={{64,0},{128,64},{192,128},{256,192},{320,256},{384,320},{448,384},... | collective-permute-start | bytes 393224 | tf_op jit(solution)/shard_map/ppermute | solution.py:286
  38.7 6.9 %collective-permute-start.2 = (bf16[16,32,128]{2,1,0:T(8,128)(2,1)S(1)}, bf16[16,32,128]{2,1,0:T(8,128)(2,1)S(1)}, u32[]{:S(2)}, u32[]{:S(2)}) collective-permute-start(bf16[16,32,128]{2,1,0:T(8,128)(2,1)S(1)} %pad_maximum_fusion.own), channel_id=1, source_target_pairs={{128,0},{448,64},{256,128},{64,192},{384,256},{192,320},{0,384},{3... | collective-permute-start | bytes 393224 | tf_op jit(solution)/shard_map/ppermute | solution.py:309
  49.8 13.1 %copy-start = (bf16[1,64,3,4096]{3,1,2,0:T(8,128)(2,1)S(1)}, bf16[1,64,3,4096]{3,1,2,0:T(8,128)(2,1)}, u32[]{:S(2)}) copy-start(bf16[1,64,3,4096]{3,1,2,0:T(8,128)(2,1)} %param.7) | copy-start | bytes 4718596
  49.8 13.1 %copy-start.3 = (f32[3,3,4096]{2,1,0:T(4,128)S(1)}, f32[3,3,4096]{2,1,0:T(4,128)}, u32[]{:S(2)}) copy-start(f32[3,3,4096]{2,1,0:T(4,128)} %weights.1) | copy-start | bytes 442372
  55.4 25.3 %all-to-all-start.1 = ((bf16[64,32,128]{2,1,0:T(8,128)(2,1)}), bf16[64,32,128]{2,1,0:T(8,128)(2,1)S(1)}, u32[]{:S(2)}, u32[]{:S(2)}) async-start(bf16[64,32,128]{2,1,0:T(8,128)(2,1)} %convolve.1), calls=%async_computation.1 | async-start | bytes 1048576 | tf_op jit(solution)/shard_map/all_to_all | solution.py:351

commit v5 on v4

--- a/solution.py
+++ b/solution.py
@@ -183,12 +183,17 @@
         copy.wait()
 
 
-def turn_filter_kernel(filt, out):
-    for i in range(out.shape[0] // 2):
+def head_kernel(parts, filt_in, own, last, tail, filt, sems):
+    rows = tail.shape[1]
+    made = copies([(parts.at[:, pl.ds(parts.shape[1] - rows, rows), :], tail), (filt_in, filt)], sems)
+    made[0].wait()
+    last[...] = tail[:, rows - 2 :, :]
+    made[1].wait()
+    for i in range(own.shape[0] // 2):
         block = filt[:, i * 128 : (i + 1) * 128].T
         for j in range(2):
             part = block[j * 64 : (j + 1) * 64]
-            out[2 * i + j] = jnp.concatenate([part[:32], part[32:]], axis=1).astype(BF16)
+            own[2 * i + j] = jnp.concatenate([part[:32], part[32:]], axis=1).astype(BF16)
 
 
 def short_sum(x, halo, weights, alive):
@@ -256,7 +261,7 @@
 
 
 def params(limit):
-    return pltpu.CompilerParams(vmem_limit_bytes=limit * 1024 * 1024)
+    return pltpu.CompilerParams(vmem_limit_bytes=int(limit * 1024 * 1024))
 
 
 def per_device(rows, lengths, short_weight, long_filter, filter_bias):
@@ -269,24 +274,32 @@
     span = long_filter.shape[1]
     parts = jnp.transpose(rows[0], (1, 0, 2))
     alive = lengths - me * tok
-    halo = lax.ppermute(parts[:, tok - 2 :, :], "seq", [(i, i + 1) for i in range(nseq - 1)])
     mats, turns = [jnp.asarray(t) for t in transform_tables(nseq, tok)]
 
-    own = pl.pallas_call(
-        turn_filter_kernel,
-        out_shape=jax.ShapeDtypeStruct((span // tok, half, 2 * chans), BF16),
-        in_specs=vmem(1),
-        out_specs=pl.BlockSpec(memory_space=pltpu.VMEM),
-        compiler_params=params(24),
-        name="turn_filter",
-    )(long_filter)
+    hbm = pl.BlockSpec(memory_space=pltpu.HBM)
+    own, last = pl.pallas_call(
+        head_kernel,
+        out_shape=(
+            jax.ShapeDtypeStruct((span // tok, half, 2 * chans), BF16),
+            jax.ShapeDtypeStruct((3, 2, width), BF16),
+        ),
+        in_specs=[hbm] * 2,
+        out_specs=tuple(vmem(2)),
+        scratch_shapes=[
+            pltpu.VMEM((3, 16, width), BF16),
+            pltpu.VMEM(long_filter.shape, F32),
+            pltpu.SemaphoreType.DMA((2,)),
+        ],
+        compiler_params=params(53.75),
+        name="head",
+    )(parts, long_filter)
+    halo = lax.ppermute(last, "seq", [(i, i + 1) for i in range(nseq - 1)])
     group = lax.axis_index("grp")
 
     def from_shift(x, shift):
         return lax.ppermute(x, "grp", [((i + shift) % ngrp, i) for i in range(ngrp)])
 
     two = jnp.concatenate([own, from_shift(own, 4)], axis=0)
-    hbm = pl.BlockSpec(memory_space=pltpu.HBM)
     block = 1024
     z = pl.pallas_call(
         gate_kernel,
@@ -300,7 +313,7 @@
             pltpu.SemaphoreType.DMA((5,)),
             pltpu.SemaphoreType.DMA((4,)),
         ],
-        compiler_params=params(53),
+        compiler_params=params(53.75),
         cost_estimate=pl.CostEstimate(flops=1000000000, bytes_accessed=2000000, transcendentals=0),
         name="gate",
     )(alive, parts, halo, short_weight)

time: 82.1 us -> 81.2 us (0.989)
  local copies, waits for them, and re-layouts: 2.86 us -> 0.02 us
  starting transfers between devices: 43.8 us -> 45.9 us
  waiting for transfers between devices: 23.6 us -> 22.5 us
  Pallas kernels: 10.5 us -> 11.5 us
    unnamed x12 -> x8, local copies, waits for them, and re-layouts: 1.88 us -> 0.02 us
    all_to_all x1, waiting for transfers between devices: 4.2 us -> 2.95 us  [per_device(): z = lax.all_to_all(z, 'seq', split_axis=0, concat_axis=0, tiled=True)]
    ppermute x3, starting transfers between devices: 17.2 us -> 18.3 us  [from_shift(): lax.ppermute(x, 'grp', [((i + shift) % ngrp, i) for i in range(ngrp)])]
    all_to_all x1, starting transfers between devices: 7.55 us -> 8.62 us  [per_device(): y = lax.all_to_all(y, 'seq', split_axis=0, concat_axis=0, tiled=True)]
    pallas_call x1, Pallas kernels: 0.21 us -> 1.26 us  [per_device(): pl.pallas_call(head_kernel, out_shape=(jax.ShapeDtypeStruct((span // tok,...]
    slice x1 -> x0, local copies, waits for them, and re-layouts: 0.98 us -> none  [per_device(): parts[:, tok - 2:, :]]
where the time goes in v5:
time: 81.2 us; the launch traced here: 80.8 us
  starting transfers between devices  45.9 us (57%)
  waiting for transfers between devices  22.5 us (28%)
  Pallas kernels  11.5 us (14%)
  between operations  0.83 us (1%)
    ppermute x3, starting transfers between devices, from_shift(): lax.ppermute(x, 'grp', [((i + shift) % ngrp, i) for i in range(ngrp)])  18.3 us
    all_to_all x1, waiting for transfers between devices, per_device(): y = lax.all_to_all(y, 'seq', split_axis=0, concat_axis=0, tiled=True)  17 us
    all_to_all x1, starting transfers between devices, per_device(): z = lax.all_to_all(z, 'seq', split_axis=0, concat_axis=0, tiled=True)  9.95 us
    all_to_all x1, starting transfers between devices, per_device(): y = lax.all_to_all(y, 'seq', split_axis=0, concat_axis=0, tiled=True)  8.62 us
    pallas_call x1, Pallas kernels, per_device(): pl.pallas_call(conv_kernel, out_shape=jax.ShapeDtypeStruct((nseq, half, 2...  5.53 us
    ppermute x1, starting transfers between devices, per_device(): lax.ppermute(two, 'grp', across)  4.56 us
    ppermute x1, starting transfers between devices, per_device(): halo = lax.ppermute(last, 'seq', [(i, i + 1) for i in range(nseq - 1)])  4.51 us
    pallas_call x1, Pallas kernels, per_device(): pl.pallas_call(gate_kernel, out_shape=jax.ShapeDtypeStruct((nseq, half, 2...  3.1 us
  transfers between devices with their start and end apart: 7, of which 3 were waited for; matrix products, arithmetic and copies ran while one was open for 0% of the time, Pallas kernels for 5%

profile of v5, /device:TPU:1, one launch (start us, length us, event | category | flops | bytes accessed | tf_op | source)
XLA Modules:
  0.0 80.8 jit_solution(8455715732301807058)
XLA Ops:
  0.0 1.3 %head.1 = (bf16[8,32,128]{2,1,0:T(8,128)(2,1)S(1)}, bf16[3,2,4096]{2,1,0:T(2,128)(2,1)S(1)}) custom-call(bf16[3,64,4096]{2,1,0:T(8,128)(2,1)} %bitcast.7, f32[64,512]{1,0:T(8,128)} %filt_in.1), custom_call_target="tpu_custom_call" | custom-call | tf_op jit(solution)/shard_map/head/pallas_call | solution.py:280
  1.3 4.5 %collective-permute-start = (bf16[3,2,4096]{2,1,0:T(2,128)(2,1)S(1)}, bf16[3,2,4096]{2,1,0:T(2,128)(2,1)S(1)}, u32[]{:S(2)}, u32[]{:S(2)}) collective-permute-start(bf16[3,2,4096]{2,1,0:T(2,128)(2,1)S(1)} %get-tuple-element.9), channel_id=1, source_target_pairs={{0,1},{1,2},{2,3},{3,4},{4,5},{5,6},{6,7},{7,8},{8,9},{9,10},{10,1... | collective-permute-start | bytes 147464 | tf_op jit(solution)/shard_map/ppermute | solution.py:296
  5.8 10.6 %collective-permute-start.1 = (bf16[8,32,128]{2,1,0:T(8,128)(2,1)S(1)}, bf16[8,32,128]{2,1,0:T(8,128)(2,1)S(1)}, u32[]{:S(2)}, u32[]{:S(2)}) collective-permute-start(bf16[8,32,128]{2,1,0:T(8,128)(2,1)S(1)} %get-tuple-element.10), channel_id=1, source_target_pairs={{256,0},{320,64},{384,128},{448,192},{0,256},{64,320},{128,384},{1... | collective-permute-start | bytes 196616 | tf_op jit(solution)/shard_map/ppermute | solution.py:300
  17.1 0.0 copy-start.1
  17.1 0.0 copy-start.3
  17.1 0.0 collective-permute-done.halo
  17.1 3.1 %gate.1 = bf16[64,32,128]{2,1,0:T(8,128)(2,1)} custom-call(s32[1]{0:T(128)S(6)} %sub.7.alive, bf16[3,64,4096]{2,1,0:T(8,128)(2,1)} %bitcast.8, bf16[3,2,4096]{2,1,0:T(2,128)(2,1)S(1)} %collective-permute-done.halo, f32[3,3,4096]{2,1,0:T(4,128)} %weights.1), custom_call_target="tpu_custom_call" | custom-call | flops 1000000000 | bytes 2000000 | tf_op jit(solution)/shard_map/gate/pallas_call | solution.py:304
  20.2 0.0 collective-permute-done.1
  20.3 9.9 %all-to-all-start = ((bf16[64,32,128]{2,1,0:T(8,128)(2,1)}), bf16[64,32,128]{2,1,0:T(8,128)(2,1)S(1)}, u32[]{:S(2)}, u32[]{:S(2)}) async-start(bf16[64,32,128]{2,1,0:T(8,128)(2,1)} %gate.1), calls=%async_computation | async-start | bytes 1048576 | tf_op jit(solution)/shard_map/all_to_all | solution.py:323
  30.2 3.1 %collective-permute-start.4 = (bf16[16,32,128]{2,1,0:T(8,128)(2,1)S(1)}, bf16[16,32,128]{2,1,0:T(8,128)(2,1)S(1)}, u32[]{:S(2)}, u32[]{:S(2)}) collective-permute-start(bf16[16,32,128]{2,1,0:T(8,128)(2,1)S(1)} %pad_maximum_fusion.own), channel_id=1, source_target_pairs={{448,0},{0,64},{64,128},{128,192},{192,256},{256,320},{320,384},{3... | collective-permute-start | bytes 393224 | tf_op jit(solution)/shard_map/ppermute | solution.py:300
  33.3 4.6 %collective-permute-start.3 = (bf16[16,32,128]{2,1,0:T(8,128)(2,1)S(1)}, bf16[16,32,128]{2,1,0:T(8,128)(2,1)S(1)}, u32[]{:S(2)}, u32[]{:S(2)}) collective-permute-start(bf16[16,32,128]{2,1,0:T(8,128)(2,1)S(1)} %pad_maximum_fusion.own), channel_id=1, source_target_pairs={{64,0},{128,64},{192,128},{256,192},{320,256},{384,320},{448,384},... | collective-permute-start | bytes 393224 | tf_op jit(solution)/shard_map/ppermute | solution.py:300
  37.9 4.6 %collective-permute-start.2 = (bf16[16,32,128]{2,1,0:T(8,128)(2,1)S(1)}, bf16[16,32,128]{2,1,0:T(8,128)(2,1)S(1)}, u32[]{:S(2)}, u32[]{:S(2)}) collective-permute-start(bf16[16,32,128]{2,1,0:T(8,128)(2,1)S(1)} %pad_maximum_fusion.own), channel_id=1, source_target_pairs={{128,0},{448,64},{256,128},{64,192},{384,256},{192,320},{0,384},{3... | collective-permute-start | bytes 393224 | tf_op jit(solution)/shard_map/ppermute | solution.py:322
  42.5 0.0 collective-permute-done.4.one_back
  42.5 0.0 collective-permute-done.3.one_on
  42.5 2.5 %collective-permute-done.2.across = bf16[16,32,128]{2,1,0:T(8,128)(2,1)S(1)} collective-permute-done((bf16[16,32,128]{2,1,0:T(8,128)(2,1)S(1)}, bf16[16,32,128]{2,1,0:T(8,128)(2,1)S(1)}, u32[]{:S(2)}, u32[]{:S(2)}) %collective-permute-start.2) | collective-permute-done | bytes 131104 | tf_op jit(solution)/shard_map/ppermute | solution.py:322
  45.0 2.9 %all-to-all-done.z = bf16[64,32,128]{2,1,0:T(8,128)(2,1)S(1)} async-done(((bf16[64,32,128]{2,1,0:T(8,128)(2,1)}), bf16[64,32,128]{2,1,0:T(8,128)(2,1)S(1)}, u32[]{:S(2)}, u32[]{:S(2)}) %all-to-all-start) | async-done | bytes 524320 | tf_op jit(solution)/shard_map/all_to_all | solution.py:323
  47.9 0.0 copy-done.1
  47.9 0.0 copy-done.3
  47.9 0.0 copy-start
  47.9 0.0 copy-start.2
  47.9 5.5 %convolve.1 = bf16[64,32,128]{2,1,0:T(8,128)(2,1)} custom-call(s32[1]{0:T(128)} %bitcast.place, bf16[16,32,128]{2,1,0:T(8,128)(2,1)S(1)} %pad_maximum_fusion.own, bf16[16,32,128]{2,1,0:T(8,128)(2,1)S(1)} %collective-permute-done.2.across, bf16[16,32,128]{2,1,0:T(8,128)(2,1)S(1)} %collective-permute-done.3.one_on, ...), custom_call_target="tpu_custom_call" | custom-call | tf_op jit(solution)/shard_map/convolve/pallas_call | solution.py:346
  53.5 8.6 %all-to-all-start.1 = ((bf16[64,32,128]{2,1,0:T(8,128)(2,1)}), bf16[64,32,128]{2,1,0:T(8,128)(2,1)S(1)}, u32[]{:S(2)}, u32[]{:S(2)}) async-start(bf16[64,32,128]{2,1,0:T(8,128)(2,1)} %convolve.1), calls=%async_computation.1 | async-start | bytes 1048576 | tf_op jit(solution)/shard_map/all_to_all | solution.py:364
  62.1 0.0 copy-done
  62.1 0.0 copy-done.2
  62.1 0.6 query.1
  62.8 17.0 %all-to-all-done.1.y = bf16[64,32,128]{2,1,0:T(8,128)(2,1)S(1)} async-done(((bf16[64,32,128]{2,1,0:T(8,128)(2,1)}), bf16[64,32,128]{2,1,0:T(8,128)(2,1)S(1)}, u32[]{:S(2)}, u32[]{:S(2)}) %all-to-all-start.1) | async-done | bytes 524320 | tf_op jit(solution)/shard_map/all_to_all | solution.py:364
  79.8 1.0 %mix.1 = bf16[64,4096]{1,0:T(8,128)(2,1)} custom-call(bf16[64,32,128]{2,1,0:T(8,128)(2,1)S(1)} %all-to-all-done.1.y, f32[64,4096]{1,0:T(8,128)S(1)} %query.1), custom_call_target="tpu_custom_call" | custom-call | tf_op jit(solution)/shard_map/mix/pallas_call | solution.py:366
  (1 shorter events, 0.0 us)
Async XLA Ops:
  1.3 15.8 %collective-permute-start = (bf16[3,2,4096]{2,1,0:T(2,128)(2,1)S(1)}, bf16[3,2,4096]{2,1,0:T(2,128)(2,1)S(1)}, u32[]{:S(2)}, u32[]{:S(2)}) collective-permute-start(bf16[3,2,4096]{2,1,0:T(2,128)(2,1)S(1)} %get-tuple-element.9), channel_id=1, source_target_pairs={{0,1},{1,2},{2,3},{3,4},{4,5},{5,6},{6,7},{7,8},{8,9},{9,10},{10,1... | collective-permute-start | bytes 147464 | tf_op jit(solution)/shard_map/ppermute | solution.py:296
  5.8 14.4 %collective-permute-start.1 = (bf16[8,32,128]{2,1,0:T(8,128)(2,1)S(1)}, bf16[8,32,128]{2,1,0:T(8,128)(2,1)S(1)}, u32[]{:S(2)}, u32[]{:S(2)}) collective-permute-start(bf16[8,32,128]{2,1,0:T(8,128)(2,1)S(1)} %get-tuple-element.10), channel_id=1, source_target_pairs={{256,0},{320,64},{384,128},{448,192},{0,256},{64,320},{128,384},{1... | collective-permute-start | bytes 196616 | tf_op jit(solution)/shard_map/ppermute | solution.py:300
  17.1 30.8 %copy-start.1 = (bf16[448,256]{1,0:T(8,128)(2,1)S(1)}, bf16[448,256]{1,0:T(8,128)(2,1)}, u32[]{:S(2)}) copy-start(bf16[448,256]{1,0:T(8,128)(2,1)} %constant.15.clone.mats_in) | copy-start | bytes 688132
  17.1 30.8 %copy-start.3 = (f32[64]{0:T(128)S(1)}, f32[64]{0:T(128)}, u32[]{:S(2)}) copy-start(f32[64]{0:T(128)} %param.11) | copy-start | bytes 772
  20.3 27.7 %all-to-all-start = ((bf16[64,32,128]{2,1,0:T(8,128)(2,1)}), bf16[64,32,128]{2,1,0:T(8,128)(2,1)S(1)}, u32[]{:S(2)}, u32[]{:S(2)}) async-start(bf16[64,32,128]{2,1,0:T(8,128)(2,1)} %gate.1), calls=%async_computation | async-start | bytes 1048576 | tf_op jit(solution)/shard_map/all_to_all | solution.py:323
  30.2 12.3 %collective-permute-start.4 = (bf16[16,32,128]{2,1,0:T(8,128)(2,1)S(1)}, bf16[16,32,128]{2,1,0:T(8,128)(2,1)S(1)}, u32[]{:S(2)}, u32[]{:S(2)}) collective-permute-start(bf16[16,32,128]{2,1,0:T(8,128)(2,1)S(1)} %pad_maximum_fusion.own), channel_id=1, source_target_pairs={{448,0},{0,64},{64,128},{128,192},{192,256},{256,320},{320,384},{3... | collective-permute-start | bytes 393224 | tf_op jit(solution)/shard_map/ppermute | solution.py:300
  33.3 9.2 %collective-permute-start.3 = (bf16[16,32,128]{2,1,0:T(8,128)(2,1)S(1)}, bf16[16,32,128]{2,1,0:T(8,128)(2,1)S(1)}, u32[]{:S(2)}, u32[]{:S(2)}) collective-permute-start(bf16[16,32,128]{2,1,0:T(8,128)(2,1)S(1)} %pad_maximum_fusion.own), channel_id=1, source_target_pairs={{64,0},{128,64},{192,128},{256,192},{320,256},{384,320},{448,384},... | collective-permute-start | bytes 393224 | tf_op jit(solution)/shard_map/ppermute | solution.py:300
  37.9 7.1 %collective-permute-start.2 = (bf16[16,32,128]{2,1,0:T(8,128)(2,1)S(1)}, bf16[16,32,128]{2,1,0:T(8,128)(2,1)S(1)}, u32[]{:S(2)}, u32[]{:S(2)}) collective-permute-start(bf16[16,32,128]{2,1,0:T(8,128)(2,1)S(1)} %pad_maximum_fusion.own), channel_id=1, source_target_pairs={{128,0},{448,64},{256,128},{64,192},{384,256},{192,320},{0,384},{3... | collective-permute-start | bytes 393224 | tf_op jit(solution)/shard_map/ppermute | solution.py:322
  47.9 14.2 %copy-start = (bf16[1,64,3,4096]{3,1,2,0:T(8,128)(2,1)S(1)}, bf16[1,64,3,4096]{3,1,2,0:T(8,128)(2,1)}, u32[]{:S(2)}) copy-start(bf16[1,64,3,4096]{3,1,2,0:T(8,128)(2,1)} %param.7) | copy-start | bytes 4718596
  47.9 14.2 %copy-start.2 = (f32[3,3,4096]{2,1,0:T(4,128)S(1)}, f32[3,3,4096]{2,1,0:T(4,128)}, u32[]{:S(2)}) copy-start(f32[3,3,4096]{2,1,0:T(4,128)} %weights.1) | copy-start | bytes 442372
  53.5 26.3 %all-to-all-start.1 = ((bf16[64,32,128]{2,1,0:T(8,128)(2,1)}), bf16[64,32,128]{2,1,0:T(8,128)(2,1)S(1)}, u32[]{:S(2)}, u32[]{:S(2)}) async-start(bf16[64,32,128]{2,1,0:T(8,128)(2,1)} %convolve.1), calls=%async_computation.1 | async-start | bytes 1048576 | tf_op jit(solution)/shard_map/all_to_all | solution.py:364
